TPU v7x, 32 devices: a whole 2x2x4 slice. The times are simulated.
32 devices in a mesh: tm: 8 (over z, y), mark: 4 (over x, core).
Axes of the slice: x: 2, y: 2, z: 4, core: 2. Of those that a mesh axis runs over, the one named last changes fastest.
Arguments:
- event_marks: int32 [32768], P('tm'), may hold values from 0 to 8191
- event_gaps: int32 [32768], P('tm'), may hold values from 1 to 65536, as said below
- excite: bfloat16 [512, 8192], P('mark'), may hold values from 0 to 0.59765625
- source: bfloat16 [512, 8192], P('mark'), may hold values from 0 to 0.59765625
- base_rate: float32 [8192], replicated, may hold values from 0.05 to 0.5
- weights: float32 [8], replicated, may hold values from 0.2 to 2
- decay_rates: float32 [8], replicated, may hold values from 1.0172526041666667e-06 to 0.06666667
Outputs:
- grad_excite: float32 [512, 8192], P('mark', 'tm')
- grad_source: float32 [512, 8192], P('mark', 'tm')
- grad_base: float32 [8192], P('tm')
Inputs may be any that keep to these rules, and one draw needn't show every extreme that they name: `event_gaps`: ticks since the previous event, the first counted from time 0.
All inputs are finite; a program needn't handle non-finite values.
Results may differ from a plain program's by a relative error of at most 0.0003.
Values sent between devices are 32-bit elements; how exact they have to be, the bound alone decides.
A program may use at most 64 MiB of HBM per device.

v0:
```python
import jax
import jax.numpy as jnp
from jax import lax
from jax.sharding import PartitionSpec as P


def passed_along(array, axis, by):
    peers = lax.axis_size(axis)
    pairs = [(i, i + by) for i in range(peers) if 0 <= i + by < peers]
    return lax.ppermute(array, axis, pairs)


def decay_kernel(stamp_block, weights, decay_rates):
    block_size = stamp_block.shape[0]
    elapsed = jnp.maximum(stamp_block[:, None] - stamp_block[None, :], 0.0)
    causal = lax.broadcasted_iota(jnp.int32, (block_size, block_size), 0) > lax.broadcasted_iota(
        jnp.int32, (block_size, block_size), 1
    )
    accumulated = jnp.zeros((block_size, block_size), jnp.float32)
    for channel in range(decay_rates.shape[0]):
        accumulated = accumulated + weights[channel] * decay_rates[channel] * jnp.exp(
            -decay_rates[channel] * elapsed
        )
    return jnp.where(causal, accumulated, 0.0)


def carry_forward(summary, duration, decay_rates):

    def combine(earlier, later):
        return (
            earlier[0] * jnp.exp(-decay_rates[:, None] * later[1]) + later[0],
            earlier[1] + later[1],
        )

    empty_state = (jnp.zeros(summary.shape, jnp.float32), jnp.zeros((), jnp.float32))

    def advance(hop_index, received):
        return passed_along(combine(received, (summary, duration)), "tm", 1)

    arrived = lax.fori_loop(0, lax.axis_size("tm") - 1, advance, empty_state)
    return arrived[0]


def carry_backward(summary, duration, decay_rates):

    def combine(earlier, later):
        return (
            earlier[0] * jnp.exp(-decay_rates[:, None] * later[1]) + later[0],
            earlier[1] + later[1],
        )

    empty_state = (jnp.zeros(summary.shape, jnp.float32), jnp.zeros((), jnp.float32))

    def advance(hop_index, received):
        return passed_along(combine(received, (summary, duration)), "tm", -1)

    arrived = lax.fori_loop(0, lax.axis_size("tm") - 1, advance, empty_state)
    return arrived


def body(event_marks, event_gaps, excite, source, base_rate, weights, decay_rates):
    highest = lax.Precision.HIGHEST
    events = event_marks.shape[0]
    slices = excite.shape[0]
    mark_count = excite.shape[1]
    dense_coupling = slices * lax.axis_size("mark")
    total_events = events * lax.axis_size("tm")
    channels = decay_rates.shape[0]
    block_size = 512
    block_count = events // block_size
    stamps = jnp.cumsum(event_gaps).astype(jnp.float32)
    duration = stamps[-1]
    anchors = jnp.concatenate(
        [jnp.zeros((1,), jnp.float32), stamps[block_size - 1 :: block_size][:-1]]
    )
    stamp_blocks = stamps.reshape(block_count, block_size)
    source_rows = jnp.take(source, event_marks, axis=1).T
    excite_rows = jnp.take(excite, event_marks, axis=1).T
    source_blocks = source_rows.reshape(block_count, block_size, slices)
    excite_blocks = excite_rows.reshape(block_count, block_size, slices)

    def forward_block(carried, pieces):
        stamp_block, row_block, anchor = pieces
        values = row_block.astype(jnp.float32)
        kernel = decay_kernel(stamp_block, weights, decay_rates)
        arrival = weights[None, :] * jnp.exp(
            -decay_rates[None, :] * (stamp_block - anchor)[:, None]
        )
        inside = jnp.dot(kernel, values, precision=highest) + jnp.dot(
            arrival, carried, precision=highest
        )
        end_time = stamp_block[-1]
        emission = decay_rates[:, None] * jnp.exp(
            -decay_rates[:, None] * (end_time - stamp_block)[None, :]
        )
        carried = jnp.exp(-decay_rates * (end_time - anchor))[:, None] * carried + jnp.dot(
            emission, values, precision=highest
        )
        return (carried, inside)

    start_state = jnp.zeros((channels, slices), jnp.float32)
    emission_all = decay_rates[:, None] * jnp.exp(
        -decay_rates[:, None] * (duration - stamps)[None, :]
    )
    summary = jnp.dot(emission_all, source_rows.astype(jnp.float32), precision=highest)
    state_in = carry_forward(summary, duration, decay_rates)
    final_state, inside_blocks = lax.scan(
        forward_block, start_state, (stamp_blocks, source_blocks, anchors)
    )
    arrival_all = weights[None, :] * jnp.exp(-decay_rates[None, :] * stamps[:, None])
    excitation = inside_blocks.reshape(events, slices) + jnp.dot(
        arrival_all, state_in, precision=highest
    )
    partial_value = jnp.sum(excite_rows.astype(jnp.float32) * excitation, axis=1) / dense_coupling
    intensity = jnp.take(base_rate, event_marks) + lax.psum(partial_value, "mark")
    inverse = 1.0 / intensity
    excite_term = jax.ops.segment_sum(
        inverse[:, None] * excitation, event_marks, num_segments=mark_count
    )
    base_term = jax.ops.segment_sum(inverse, event_marks, num_segments=mark_count)
    excite_part, base_part = (
        lax.psum_scatter(excite_term.T, "tm", scatter_dimension=1, tiled=True),
        lax.psum_scatter(base_term, "tm", scatter_dimension=0, tiled=True),
    )

    def backward_block(pending, pieces):
        stamp_block, row_block, anchor, inverse_block = pieces
        weighted = inverse_block[:, None] * row_block.astype(jnp.float32)
        kernel = decay_kernel(stamp_block, weights, decay_rates)
        end_time = stamp_block[-1]
        reaching = weights[None, :] * jnp.exp(
            -decay_rates[None, :] * (end_time - stamp_block)[:, None]
        )
        inside = jnp.dot(kernel.T, weighted, precision=highest) + jnp.dot(
            reaching, pending, precision=highest
        )
        emission = decay_rates[:, None] * jnp.exp(
            -decay_rates[:, None] * (stamp_block - anchor)[None, :]
        )
        pending = jnp.exp(-decay_rates * (end_time - anchor))[:, None] * pending + jnp.dot(
            emission, weighted, precision=highest
        )
        return (pending, inside)

    inverse_blocks = inverse.reshape(block_count, block_size)
    emission_all = decay_rates[:, None] * jnp.exp(-decay_rates[:, None] * stamps[None, :])
    summary_back = jnp.dot(
        emission_all, inverse[:, None] * excite_rows.astype(jnp.float32), precision=highest
    )
    hold_in, suffix = carry_backward(summary_back, duration, decay_rates)
    final_hold, back_blocks = lax.scan(
        backward_block,
        start_state,
        (stamp_blocks, excite_blocks, anchors, inverse_blocks),
        reverse=True,
    )
    reaching_all = weights[None, :] * jnp.exp(-decay_rates[None, :] * (duration - stamps)[:, None])
    feedback = back_blocks.reshape(events, slices) + jnp.dot(
        reaching_all, hold_in, precision=highest
    )
    remaining = duration - stamps + suffix
    remainder = jnp.sum(
        weights[None, :] * (1.0 - jnp.exp(-decay_rates[None, :] * remaining[:, None])), axis=1
    )
    excite_total = jnp.sum(excite, axis=1, dtype=jnp.float32)
    source_term = jax.ops.segment_sum(
        feedback - remainder[:, None] * excite_total[None, :] / mark_count,
        event_marks,
        num_segments=mark_count,
    )
    comp_local = jnp.dot(remainder, source_rows.astype(jnp.float32), precision=highest)
    factor = mark_count / total_events
    source_part = lax.psum_scatter(source_term.T, "tm", scatter_dimension=1, tiled=True)
    comp_total, end_time = lax.psum((comp_local, duration), "tm")
    grad_excite = factor * excite_part - comp_total[:, None] / total_events
    grad_base = factor * base_part - end_time / total_events
    grad_source = factor * source_part
    return (grad_excite, grad_source, grad_base)


def solution(mesh):
    return jax.shard_map(
        body,
        mesh=mesh,
        in_specs=(P("tm"), P("tm"), P("mark", None), P("mark", None), P(), P(), P()),
        out_specs=(P("mark", "tm"), P("mark", "tm"), P("tm")),
        check_vma=False,
    )
```

profile of v0, /device:TPU:0, one launch (start us, length us, event | category | flops | bytes accessed | tf_op | source)
XLA Modules:
  0.0 515.8 jit_solution(17530908629876625945)
XLA Ops:
  31.4 23.0 %gather_fusion = f32[4096]{0:T(1024)S(1)} fusion(f32[8192]{0:T(1024)S(1)} %copy-done, s32[4096]{0:T(1024)S(1)} %fusion.197), kind=kCustom, calls=%fused_computation.2 | custom fusion | bytes 49152 | tf_op jit(solution)/shard_map/jit(_take)/gather | solution.py:115
  54.4 14.9 %gather_fusion.2 = bf16[4096,128]{1,0:T(8,128)(2,1)} fusion(bf16[128,8192]{0,1:T(8,128)(2,1)S(1)} %copy.46, s32[4096]{0:T(1024)S(1)} %fusion.197), kind=kCustom, calls=%fused_computation.1.clone | custom fusion | bytes 2113536 | tf_op jit(solution)/shard_map/jit(_take)/gather | solution.py:77
  72.6 12.1 %gather_fusion.1 = bf16[4096,128]{1,0:T(8,128)(2,1)S(1)} fusion(bf16[128,8192]{0,1:T(8,128)(2,1)S(1)} %copy.43, s32[4096]{0:T(1024)S(1)} %fusion.197), kind=kCustom, calls=%fused_computation.clone | custom fusion | bytes 2113536 | tf_op jit(solution)/shard_map/jit(_take)/gather | solution.py:78
  88.5 49.1 %while.61 = (s32[]{:T(128)}, f32[8,128]{1,0:T(8,128)S(1)}, f32[8,512,128]{2,1,0:T(8,128)S(1)}, f32[8,1]{0,1:T(1,128)S(1)}, f32[8,512]{1,0:T(8,128)S(1)}, /*index...) while((s32[]{:T(128)}, f32[8,128]{1,0:T(8,128)S(1)}, ...), condition=%wide.region_3.5_spmd.clone, body=%wide.region_2.4_spmd.clone.sunk | while | flops 422401024 | bytes 1082332 | solution.py:107
  140.1 47.3 %while.59 = (s32[]{:T(128)}, f32[8,128]{1,0:T(8,128)S(1)}, f32[]{:T(128)}, f32[8,1]{0,1:T(1,128)S(1)}, f32[8,128]{1,0:T(8,128)S(1)}, /*index=5*/s32[]{:T(128)}) while((s32[]{:T(128)}, f32[8,128]{1,0:T(8,128)S(1)}, f32[]{:T(128)}, f32[8,1]{0,1:T(1,128)S(1)}, f32[8,128]{1,0:T(8,128)S(1)}, /*index=5*/s32[]{:T(128)}) %tuple.177), condition=%wide.region_5.7_spmd, body=%wide.region_4.6_spmd.sunk | while | flops 2058 | bytes 28881 | solution.py:40
  159.9 5.1 collective-permute-start
  166.9 5.1 collective-permute-start
  187.3 5.8 %fusion.161 = (f32[4096]{0:T(1024)S(1)}, bf16[4096,128]{0,1:T(8,128)(2,1)}, f32[4096,128]{0,1:T(8,128)}) fusion(bf16[4096,128]{0,1:T(8,128)(2,1)} %copy.44, pred[4096]{0:T(1024)(128)(4,1)S(1)} %compare_and_fusion, f32[4096,128]{0,1:T(8,128)} %copy.52, f32[8,128]{1,0:T(8,128)S(1)} %get-tuple-element.783, f32[4096]{0:T(1024)S(1)} %convert_bitcast_fusion, ...), kind=kOutput, calls=%fused_computation.192 | convolution fusion | flops 53014528 | bytes 6332480 | tf_op jit(solution)/shard_map/dot_general | solution.py:111
  193.1 10.1 %psum.21 = f32[4096]{0:T(1024)S(1)} all-reduce(f32[4096]{0:T(1024)S(1)} %broadcast_multiply_fusion.2), channel_id=1, replica_groups=mesh['tm'=8,'mark'=4] {'mark'}, use_global_device_ids=true, to_apply=%region_7.9 | all-reduce | flops 4096 | bytes 32768 | tf_op jit(solution)/shard_map/psum | solution.py:115
  206.9 24.8 %scatter_custom_fusion = f32[8192,128]{1,0:T(8,128)} fusion(s32[4096]{0:T(1024)S(1)} %copy-done.4, f32[4096,128]{1,0:T(8,128)} %copy.48, f32[]{:T(128)} %constant.136.clone.1), kind=kCustom, calls=%fused_computation.196 | custom fusion | flops 524288 | bytes 4194816 | tf_op jit(solution)/shard_map/scatter-add | solution.py:117
  238.9 71.9 %while.60 = (s32[]{:T(128)}, f32[8,128]{1,0:T(8,128)S(1)}, f32[]{:T(128)}, f32[]{:T(128)}, f32[8,1]{0,1:T(1,128)S(1)}, /*index=5*/f32[8,128]{1,0:T(8,128)S(1)}, s32[]{:T(128)}) while((s32[]{:T(128)}, f32[8,128]{1,0:T(8,128)S(1)}, f32[]{:T(128)}, f32[]{:T(128)}, f32[8,1]{0,1:T(1,128)S(1)}, /*index=5*/f32[8,128]{1,0:T(8,128)S(1)}, ...), condition=%wide.region_11.13_spmd, body=%wide.region_10.12_spmd.sunk | while | flops 2059 | bytes 28957 | solution.py:57
  242.7 5.9 %collective-permute-done.2 = f32[]{:T(128)} collective-permute-done((f32[]{:T(128)}, f32[]{:T(128)}, u32[]{:S(2)}, u32[]{:S(2)}) %collective-permute-start.2) | collective-permute-done | bytes 36 | tf_op jit(solution)/shard_map/while/body/eval_jaxpr/ppermute | solution.py:10
  253.0 6.5 %collective-permute-done.2 = f32[]{:T(128)} collective-permute-done((f32[]{:T(128)}, f32[]{:T(128)}, u32[]{:S(2)}, u32[]{:S(2)}) %collective-permute-start.2) | collective-permute-done | bytes 36 | tf_op jit(solution)/shard_map/while/body/eval_jaxpr/ppermute | solution.py:10
  263.9 5.8 %collective-permute-done.2 = f32[]{:T(128)} collective-permute-done((f32[]{:T(128)}, f32[]{:T(128)}, u32[]{:S(2)}, u32[]{:S(2)}) %collective-permute-start.2) | collective-permute-done | bytes 36 | tf_op jit(solution)/shard_map/while/body/eval_jaxpr/ppermute | solution.py:10
  274.1 6.0 %collective-permute-done.2 = f32[]{:T(128)} collective-permute-done((f32[]{:T(128)}, f32[]{:T(128)}, u32[]{:S(2)}, u32[]{:S(2)}) %collective-permute-start.2) | collective-permute-done | bytes 36 | tf_op jit(solution)/shard_map/while/body/eval_jaxpr/ppermute | solution.py:10
  284.4 5.6 %collective-permute-done.2 = f32[]{:T(128)} collective-permute-done((f32[]{:T(128)}, f32[]{:T(128)}, u32[]{:S(2)}, u32[]{:S(2)}) %collective-permute-start.2) | collective-permute-done | bytes 36 | tf_op jit(solution)/shard_map/while/body/eval_jaxpr/ppermute | solution.py:10
  294.5 5.6 %collective-permute-done.2 = f32[]{:T(128)} collective-permute-done((f32[]{:T(128)}, f32[]{:T(128)}, u32[]{:S(2)}, u32[]{:S(2)}) %collective-permute-start.2) | collective-permute-done | bytes 36 | tf_op jit(solution)/shard_map/while/body/eval_jaxpr/ppermute | solution.py:10
  304.5 5.6 %collective-permute-done.2 = f32[]{:T(128)} collective-permute-done((f32[]{:T(128)}, f32[]{:T(128)}, u32[]{:S(2)}, u32[]{:S(2)}) %collective-permute-start.2) | collective-permute-done | bytes 36 | tf_op jit(solution)/shard_map/while/body/eval_jaxpr/ppermute | solution.py:10
  311.6 70.3 %while.62 = (s32[]{:T(128)}, f32[8,128]{1,0:T(8,128)S(1)}, f32[8,512,128]{2,1,0:T(8,128)S(1)}, f32[8,1]{0,1:T(1,128)S(1)}, f32[8,512]{1,0:T(8,128)S(1)}, /*index...) while((s32[]{:T(128)}, f32[8,128]{1,0:T(8,128)S(1)}, ...), condition=%wide.region_15.17_spmd.clone, body=%wide.region_14.16_spmd.clone.sunk | while | flops 422663168 | bytes 1097240 | solution.py:151
  382.0 5.4 %fusion.160 = f32[4096,128]{1,0:T(8,128)} fusion(f32[4096,128]{1,0:T(8,128)S(1)} %bitcast.145, f32[8,128]{1,0:T(8,128)S(1)} %get-tuple-element.786, f32[128]{0:T(128)S(1)} %convert_reduce_fusion, f32[4096]{0:T(1024)S(1)} %multiply_reduce_fusion, f32[4096]{0:T(1024)S(1)} %broadcast_subtract_fusion.4, f32[8]{0:T(128)S(1)} %get-tuple-element.1237, ...), kind=kOutput, calls=%fused_computation.187 | convolution fusion | flops 52494336 | bytes 4231744 | tf_op jit(solution)/shard_map/dot_general | solution.py:158
  387.3 24.8 %scatter_custom_fusion.1 = f32[8192,128]{1,0:T(8,128)} fusion(s32[4096]{0:T(1024)S(1)} %copy-done.4, f32[4096,128]{1,0:T(8,128)} %fusion.160, f32[]{:T(128)} %constant.136.clone.1), kind=kCustom, calls=%fused_computation.194 | custom fusion | flops 524288 | bytes 4194816 | tf_op jit(solution)/shard_map/scatter-add | solution.py:166
  412.2 21.9 %scatter_custom_fusion.2 = f32[8192]{0:T(1024)S(1)} fusion(s32[4096]{0:T(1024)S(1)} %copy-done.4, f32[4096]{0:T(1024)S(1)} %add_divide_fusion, f32[]{:T(128)} %constant.136.clone.1), kind=kCustom, calls=%fused_computation.236 | custom fusion | flops 4096 | bytes 32772 | tf_op jit(solution)/shard_map/scatter-add | solution.py:120
  435.9 42.9 %all-reduce.1 = (f32[128]{0:T(128)S(1)}, f32[8192]{0:T(1024)S(1)}, f32[]{:T(128)}) all-reduce(f32[128]{0:T(128)S(1)} %convolution_bitcast_fusion, f32[8192]{0:T(1024)S(1)} %scatter_custom_fusion.2, f32[]{:T(128)} %bitcast.29), channel_id=1, replica_groups=mesh['tm'=8,'mark'=4] {'tm'}, use_global_device_ids=true, to_apply=%region_13.15 | all-reduce | flops 8321 | bytes 66568 | tf_op jit(solution)/shard_map/psum | solution.py:174
  482.1 24.8 %reduce-scatter.5.cloned.1.call-done = f32[128,1024]{0,1:T(8,128)} async-done(((f32[128,8192]{0,1:T(8,128)}), f32[128,1024]{0,1:T(8,128)}) %reduce-scatter.5.cloned.1.call-update) | async-done | bytes 524304 | tf_op jit(solution)/shard_map/reduce_scatter | solution.py:173
  (254 shorter events, 193.9 us)
Async XLA Ops:
  7.2 24.2 %copy-start = (f32[8192]{0:T(1024)S(1)}, f32[8192]{0:T(1024)}, u32[]{:S(2)}) copy-start(f32[8192]{0:T(1024)} %param.21) | copy-start | bytes 98308
  7.2 472.8 %reduce-scatter.3.cloned.1.call-start = ((), (), s32[]{:S(2)}) async-start(), calls=%async_computation.2 | async-start | bytes 4718592 | tf_op jit(solution)/shard_map/reduce_scatter | solution.py:122
  140.7 6.2 %collective-permute-start = (f32[8,128]{1,0:T(8,128)S(1)}, f32[8,128]{1,0:T(8,128)S(1)}, u32[]{:S(2)}, u32[]{:S(2)}) collective-permute-start(f32[8,128]{1,0:T(8,128)S(1)} %multiply_add_fusion.4), channel_id=1, source_target_pairs={{0,4},{4,8},{8,12},{12,16},{16,20},{20,24},{24,28},{1,5},{5,9},{9,... | collective-permute-start | bytes 12296 | tf_op jit(solution)/shard_map/while/body/eval_jaxpr/ppermute | solution.py:10
  147.5 5.5 %collective-permute-start = (f32[8,128]{1,0:T(8,128)S(1)}, f32[8,128]{1,0:T(8,128)S(1)}, u32[]{:S(2)}, u32[]{:S(2)}) collective-permute-start(f32[8,128]{1,0:T(8,128)S(1)} %multiply_add_fusion.4), channel_id=1, source_target_pairs={{0,4},{4,8},{8,12},{12,16},{16,20},{20,24},{24,28},{1,5},{5,9},{9,... | collective-permute-start | bytes 12296 | tf_op jit(solution)/shard_map/while/body/eval_jaxpr/ppermute | solution.py:10
  153.6 5.6 %collective-permute-start = (f32[8,128]{1,0:T(8,128)S(1)}, f32[8,128]{1,0:T(8,128)S(1)}, u32[]{:S(2)}, u32[]{:S(2)}) collective-permute-start(f32[8,128]{1,0:T(8,128)S(1)} %multiply_add_fusion.4), channel_id=1, source_target_pairs={{0,4},{4,8},{8,12},{12,16},{16,20},{20,24},{24,28},{1,5},{5,9},{9,... | collective-permute-start | bytes 12296 | tf_op jit(solution)/shard_map/while/body/eval_jaxpr/ppermute | solution.py:10
  159.9 6.4 %collective-permute-start = (f32[8,128]{1,0:T(8,128)S(1)}, f32[8,128]{1,0:T(8,128)S(1)}, u32[]{:S(2)}, u32[]{:S(2)}) collective-permute-start(f32[8,128]{1,0:T(8,128)S(1)} %multiply_add_fusion.4), channel_id=1, source_target_pairs={{0,4},{4,8},{8,12},{12,16},{16,20},{20,24},{24,28},{1,5},{5,9},{9,... | collective-permute-start | bytes 12296 | tf_op jit(solution)/shard_map/while/body/eval_jaxpr/ppermute | solution.py:10
  166.9 6.4 %collective-permute-start = (f32[8,128]{1,0:T(8,128)S(1)}, f32[8,128]{1,0:T(8,128)S(1)}, u32[]{:S(2)}, u32[]{:S(2)}) collective-permute-start(f32[8,128]{1,0:T(8,128)S(1)} %multiply_add_fusion.4), channel_id=1, source_target_pairs={{0,4},{4,8},{8,12},{12,16},{16,20},{20,24},{24,28},{1,5},{5,9},{9,... | collective-permute-start | bytes 12296 | tf_op jit(solution)/shard_map/while/body/eval_jaxpr/ppermute | solution.py:10
  173.9 6.4 %collective-permute-start = (f32[8,128]{1,0:T(8,128)S(1)}, f32[8,128]{1,0:T(8,128)S(1)}, u32[]{:S(2)}, u32[]{:S(2)}) collective-permute-start(f32[8,128]{1,0:T(8,128)S(1)} %multiply_add_fusion.4), channel_id=1, source_target_pairs={{0,4},{4,8},{8,12},{12,16},{16,20},{20,24},{24,28},{1,5},{5,9},{9,... | collective-permute-start | bytes 12296 | tf_op jit(solution)/shard_map/while/body/eval_jaxpr/ppermute | solution.py:10
  180.9 6.4 %collective-permute-start = (f32[8,128]{1,0:T(8,128)S(1)}, f32[8,128]{1,0:T(8,128)S(1)}, u32[]{:S(2)}, u32[]{:S(2)}) collective-permute-start(f32[8,128]{1,0:T(8,128)S(1)} %multiply_add_fusion.4), channel_id=1, source_target_pairs={{0,4},{4,8},{8,12},{12,16},{16,20},{20,24},{24,28},{1,5},{5,9},{9,... | collective-permute-start | bytes 12296 | tf_op jit(solution)/shard_map/while/body/eval_jaxpr/ppermute | solution.py:10
  231.7 275.2 %reduce-scatter.5.cloned.1.call-start = ((), (), s32[]{:S(2)}) async-start(), calls=%async_computation.3 | async-start | bytes 4718592 | tf_op jit(solution)/shard_map/reduce_scatter | solution.py:173
  239.5 9.0 %collective-permute-start.1 = (f32[8,128]{1,0:T(8,128)S(1)}, f32[8,128]{1,0:T(8,128)S(1)}, u32[]{:S(2)}, u32[]{:S(2)}) collective-permute-start(f32[8,128]{1,0:T(8,128)S(1)} %multiply_add_fusion.5), channel_id=1, source_target_pairs={{4,0},{8,4},{12,8},{16,12},{20,16},{24,20},{28,24},{5,1},{9,5},{13... | collective-permute-start | bytes 12296 | tf_op jit(solution)/shard_map/while/body/eval_jaxpr/ppermute | solution.py:10
  241.4 7.2 %collective-permute-start.2 = (f32[]{:T(128)}, f32[]{:T(128)}, u32[]{:S(2)}, u32[]{:S(2)}) collective-permute-start(f32[]{:T(128)} %add.392), channel_id=1, source_target_pairs={{4,0},{8,4},{12,8},{16,12},{20,16},{24,20},{28,24},{5,1},{9,5},{13... | collective-permute-start | bytes 20 | tf_op jit(solution)/shard_map/while/body/eval_jaxpr/ppermute | solution.py:10
  249.8 9.6 %collective-permute-start.1 = (f32[8,128]{1,0:T(8,128)S(1)}, f32[8,128]{1,0:T(8,128)S(1)}, u32[]{:S(2)}, u32[]{:S(2)}) collective-permute-start(f32[8,128]{1,0:T(8,128)S(1)} %multiply_add_fusion.5), channel_id=1, source_target_pairs={{4,0},{8,4},{12,8},{16,12},{20,16},{24,20},{28,24},{5,1},{9,5},{13... | collective-permute-start | bytes 12296 | tf_op jit(solution)/shard_map/while/body/eval_jaxpr/ppermute | solution.py:10
  251.7 7.8 %collective-permute-start.2 = (f32[]{:T(128)}, f32[]{:T(128)}, u32[]{:S(2)}, u32[]{:S(2)}) collective-permute-start(f32[]{:T(128)} %add.392), channel_id=1, source_target_pairs={{4,0},{8,4},{12,8},{16,12},{20,16},{24,20},{28,24},{5,1},{9,5},{13... | collective-permute-start | bytes 20 | tf_op jit(solution)/shard_map/while/body/eval_jaxpr/ppermute | solution.py:10
  260.7 8.9 %collective-permute-start.1 = (f32[8,128]{1,0:T(8,128)S(1)}, f32[8,128]{1,0:T(8,128)S(1)}, u32[]{:S(2)}, u32[]{:S(2)}) collective-permute-start(f32[8,128]{1,0:T(8,128)S(1)} %multiply_add_fusion.5), channel_id=1, source_target_pairs={{4,0},{8,4},{12,8},{16,12},{20,16},{24,20},{28,24},{5,1},{9,5},{13... | collective-permute-start | bytes 12296 | tf_op jit(solution)/shard_map/while/body/eval_jaxpr/ppermute | solution.py:10
  262.5 7.1 %collective-permute-start.2 = (f32[]{:T(128)}, f32[]{:T(128)}, u32[]{:S(2)}, u32[]{:S(2)}) collective-permute-start(f32[]{:T(128)} %add.392), channel_id=1, source_target_pairs={{4,0},{8,4},{12,8},{16,12},{20,16},{24,20},{28,24},{5,1},{9,5},{13... | collective-permute-start | bytes 20 | tf_op jit(solution)/shard_map/while/body/eval_jaxpr/ppermute | solution.py:10
  270.9 9.1 %collective-permute-start.1 = (f32[8,128]{1,0:T(8,128)S(1)}, f32[8,128]{1,0:T(8,128)S(1)}, u32[]{:S(2)}, u32[]{:S(2)}) collective-permute-start(f32[8,128]{1,0:T(8,128)S(1)} %multiply_add_fusion.5), channel_id=1, source_target_pairs={{4,0},{8,4},{12,8},{16,12},{20,16},{24,20},{28,24},{5,1},{9,5},{13... | collective-permute-start | bytes 12296 | tf_op jit(solution)/shard_map/while/body/eval_jaxpr/ppermute | solution.py:10
  272.8 7.3 %collective-permute-start.2 = (f32[]{:T(128)}, f32[]{:T(128)}, u32[]{:S(2)}, u32[]{:S(2)}) collective-permute-start(f32[]{:T(128)} %add.392), channel_id=1, source_target_pairs={{4,0},{8,4},{12,8},{16,12},{20,16},{24,20},{28,24},{5,1},{9,5},{13... | collective-permute-start | bytes 20 | tf_op jit(solution)/shard_map/while/body/eval_jaxpr/ppermute | solution.py:10
  281.3 8.8 %collective-permute-start.1 = (f32[8,128]{1,0:T(8,128)S(1)}, f32[8,128]{1,0:T(8,128)S(1)}, u32[]{:S(2)}, u32[]{:S(2)}) collective-permute-start(f32[8,128]{1,0:T(8,128)S(1)} %multiply_add_fusion.5), channel_id=1, source_target_pairs={{4,0},{8,4},{12,8},{16,12},{20,16},{24,20},{28,24},{5,1},{9,5},{13... | collective-permute-start | bytes 12296 | tf_op jit(solution)/shard_map/while/body/eval_jaxpr/ppermute | solution.py:10
  283.1 6.9 %collective-permute-start.2 = (f32[]{:T(128)}, f32[]{:T(128)}, u32[]{:S(2)}, u32[]{:S(2)}) collective-permute-start(f32[]{:T(128)} %add.392), channel_id=1, source_target_pairs={{4,0},{8,4},{12,8},{16,12},{20,16},{24,20},{28,24},{5,1},{9,5},{13... | collective-permute-start | bytes 20 | tf_op jit(solution)/shard_map/while/body/eval_jaxpr/ppermute | solution.py:10
  291.3 8.8 %collective-permute-start.1 = (f32[8,128]{1,0:T(8,128)S(1)}, f32[8,128]{1,0:T(8,128)S(1)}, u32[]{:S(2)}, u32[]{:S(2)}) collective-permute-start(f32[8,128]{1,0:T(8,128)S(1)} %multiply_add_fusion.5), channel_id=1, source_target_pairs={{4,0},{8,4},{12,8},{16,12},{20,16},{24,20},{28,24},{5,1},{9,5},{13... | collective-permute-start | bytes 12296 | tf_op jit(solution)/shard_map/while/body/eval_jaxpr/ppermute | solution.py:10
  293.2 6.9 %collective-permute-start.2 = (f32[]{:T(128)}, f32[]{:T(128)}, u32[]{:S(2)}, u32[]{:S(2)}) collective-permute-start(f32[]{:T(128)} %add.392), channel_id=1, source_target_pairs={{4,0},{8,4},{12,8},{16,12},{20,16},{24,20},{28,24},{5,1},{9,5},{13... | collective-permute-start | bytes 20 | tf_op jit(solution)/shard_map/while/body/eval_jaxpr/ppermute | solution.py:10
  301.4 8.8 %collective-permute-start.1 = (f32[8,128]{1,0:T(8,128)S(1)}, f32[8,128]{1,0:T(8,128)S(1)}, u32[]{:S(2)}, u32[]{:S(2)}) collective-permute-start(f32[8,128]{1,0:T(8,128)S(1)} %multiply_add_fusion.5), channel_id=1, source_target_pairs={{4,0},{8,4},{12,8},{16,12},{20,16},{24,20},{28,24},{5,1},{9,5},{13... | collective-permute-start | bytes 12296 | tf_op jit(solution)/shard_map/while/body/eval_jaxpr/ppermute | solution.py:10
  303.2 6.9 %collective-permute-start.2 = (f32[]{:T(128)}, f32[]{:T(128)}, u32[]{:S(2)}, u32[]{:S(2)}) collective-permute-start(f32[]{:T(128)} %add.392), channel_id=1, source_target_pairs={{4,0},{8,4},{12,8},{16,12},{20,16},{24,20},{28,24},{5,1},{9,5},{13... | collective-permute-start | bytes 20 | tf_op jit(solution)/shard_map/while/body/eval_jaxpr/ppermute | solution.py:10
  (6 other events, 44.6 us)
Sparse Core Ops, SparseCore 0:
  231.8 91.8 reduce-scatter.2
  412.3 94.5 reduce-scatter.4
where the time goes:
time: 518 us; the launch traced here: 516 us
  other arithmetic  112 us (22%)
  local copies, waits for them, and re-layouts  90.3 us (17%)
  waiting for transfers between devices  75 us (14%)
  matrix products  73.8 us (14%)
  blocking collectives  53 us (10%)
  starting transfers between devices  51.9 us (10%)
  between operations  30.7 us (6%)
  loops' own time  29.7 us (6%)
    ppermute x21, starting transfers between devices, passed_along(): return lax.ppermute(array, axis, pairs)  51.6 us
    ppermute x21, waiting for transfers between devices, passed_along(): return lax.ppermute(array, axis, pairs)  50.1 us
    psum x1, blocking collectives, body(): comp_total, end_time = lax.psum((comp_local, duration), 'tm')  42.9 us
    scatter-add x1, other arithmetic, body(): jax.ops.segment_sum(feedback - remainder[:, None] * excite_total[None, :]...  24.8 us
    reduce_scatter x1, waiting for transfers between devices, body(): lax.psum_scatter(source_term.T, 'tm', scatter_dimension=1, tiled=True)  24.8 us
    scatter-add x1, other arithmetic, body(): jax.ops.segment_sum(inverse[:, None] * excitation, event_marks, num_segme...  24.8 us
    dot_general x8, matrix products, backward_block(): jnp.dot(kernel.T, weighted, precision=highest)  24 us
    gather x1, local copies, waits for them, and re-layouts, body(): jnp.take(base_rate, event_marks) + lax.psum(partial_value, 'mark')  23 us
  transfers between devices with their start and end apart: 23, of which 15 were waited for; matrix products, arithmetic and copies ran while one was open for 24% of the time, Pallas kernels for 0%

commit v1 on v0

v1 whole, which is shorter than its diff:
```python
import functools

import jax
import jax.numpy as jnp
from jax import lax
from jax.experimental import pallas as pl
from jax.experimental.pallas import tpu as pltpu
from jax.sharding import PartitionSpec as P

F32 = jnp.float32
BF16 = jnp.bfloat16
B = 128
HIGH = lax.Precision.HIGHEST
VMEM = pl.BlockSpec(memory_space=pltpu.VMEM)
SMEM = pl.BlockSpec(memory_space=pltpu.SMEM)
NT = (((1,), (1,)), ((), ()))


def iota(shape, axis):
    return lax.broadcasted_iota(jnp.int32, shape, axis)


def split(a):
    high = a.astype(BF16)
    return high, (a - high.astype(F32)).astype(BF16)


def dot(a, b):
    return jnp.dot(a, b, preferred_element_type=F32)


def two_term(a, b):
    high, low = split(a)
    n = a.shape[0]
    both = dot(jnp.concatenate([high.astype(F32), low.astype(F32)], 0).astype(BF16), b)
    return both[:n] + both[n:]


def down(ref, count, width=B):
    row = iota((count, width), 0)
    out = jnp.zeros((count, width), F32)
    for k in range(count):
        out = jnp.where(row == k, ref[k], out)
    return out


def across(ref, count, copies):
    lane = iota((1, B), 1)
    out = jnp.zeros((1, B), F32)
    for k in range(count):
        hit = (lane < copies * count) & (lax.rem(lane, count) == k)
        out = jnp.where(hit, ref[k], out)
    return out


def columns(u):
    blocks = u.shape[0]
    return jnp.concatenate([u, jnp.zeros((B - blocks, B), F32)], 0).T


def state_rows(state):
    high, low = split(state)
    high, low = high.astype(F32), low.astype(F32)
    fill = jnp.zeros((B - 3 * state.shape[0], state.shape[1]), F32)
    return jnp.concatenate([high, low, high, fill], 0).astype(BF16)


def state_lanes(a, count):
    high, low = split(a)
    lane = iota(a.shape, 1)
    return jnp.where(lane < 2 * count, high.astype(F32), low.astype(F32)).astype(BF16)


def gather_kernel(
    count, marks, decay, gaps, src, exc, srows, xrows, u_out, sums, device, xtot, tab_s, tab_x
):
    events, width = srows.shape
    blocks = events // B

    def turn(c, total):
        s = pl.ds(pl.multiple_of(c * B, B), B)
        tab_s[s, :] = src[:, s].astype(F32).T
        t = exc[:, s].astype(F32).T
        tab_x[s, :] = t
        return total + jnp.sum(t.reshape(B // 8, 8, width), axis=0)

    total = lax.fori_loop(0, src.shape[1] // B, turn, jnp.zeros((8, width), F32))
    xtot[...] = jnp.broadcast_to(jnp.sum(total, axis=0, keepdims=True), (8, width))

    def fetch(g, _):
        for j in range(16):
            e = g * 16 + j
            m = marks[e]
            srows[pl.ds(e, 1), :] = tab_s[pl.ds(m, 1), :]
            xrows[pl.ds(e, 1), :] = tab_x[pl.ds(m, 1), :]
        return 0

    lax.fori_loop(0, events // 16, fetch, 0)
    upper = (iota((B, B), 0) <= iota((B, B), 1)).astype(F32)
    u = jnp.dot(gaps[...].astype(F32), upper, precision=HIGH, preferred_element_type=F32)
    u_out[...] = u
    d, dw = down(decay, count), down(decay, count, width)
    state = jnp.zeros((count, width), F32)
    duration = jnp.zeros((1, 1), F32)
    for b in range(blocks):
        ub = u[b : b + 1, :]
        length = ub[:, B - 1 :]
        values = srows[b * B : (b + 1) * B, :].astype(BF16)
        part = two_term(d * jnp.exp(-d * (length - ub)), values)
        sums[b * count : (b + 1) * count, :] = part
        state = state * jnp.exp(-dw * length) + part
        duration = duration + length
    device[0:count, :] = state
    device[count:, :] = jnp.broadcast_to(duration, (8, width))


def inside_kernel(count, weights, decay, u_ref, marks, base, srows, sym, inside, lanes, base_e):
    blocks = u_ref.shape[0]
    u = u_ref[...]
    ut = columns(u)
    wide_d, wide_w = across(decay, count, 3), across(weights, count, 3)
    earlier = iota((B, B), 0) > iota((B, B), 1)
    bh, bl = split(base[...])
    base2 = jnp.concatenate([bh.astype(F32), bl.astype(F32)], 0).T.astype(BF16)
    groups = base.shape[0]
    for b in range(blocks):
        col = ut[:, b : b + 1]
        row = u[b : b + 1, :]
        apart = jnp.abs(col - row)
        g = jnp.zeros((B, B), F32)
        for k in range(count):
            g = g + (weights[k] * decay[k]) * jnp.exp(-decay[k] * apart)
        s = slice(b * B, (b + 1) * B)
        sym[s, :] = g
        high, low = split(jnp.where(earlier, g, 0.0))
        values = srows[s, :].astype(BF16)
        inside[s, :] = dot(high, values) + dot(low, values)
        lanes[s, :] = state_lanes(wide_w * jnp.exp(-wide_d * col), count)
        m = marks[b : b + 1, :]
        hi, lo = m // B, lax.rem(m, B)
        pick = (lax.rem(iota((2 * groups, B), 0), groups) == hi).astype(BF16)
        found = dot(base2, pick)
        base_e[b : b + 1, :] = jnp.sum(
            jnp.where(iota((B, B), 0) == lo, found, 0.0), axis=0, keepdims=True
        )


def forward_kernel(
    count, rank, weights, decay, place, u_ref, summaries, sums, lanes, inside, srows, xrows,
    excitation, partial, remain, misc,
):
    blocks = u_ref.shape[0]
    peers = summaries.shape[0]
    me = place[0]
    u = u_ref[...]
    width = srows.shape[1]
    d, w, dw = down(decay, count), down(weights, count), down(decay, count, width)
    state = jnp.zeros((count, width), F32)
    after = jnp.zeros((1, 1), F32)
    end = jnp.zeros((1, 1), F32)
    for r in range(peers):
        length = summaries[r, count : count + 1, 0:1]
        state = jnp.where(
            r < me, state * jnp.exp(-dw * length) + summaries[r, 0:count, :], state
        )
        after = after + jnp.where(r > me, length, 0.0)
        end = end + length
    ones = jnp.ones((8, width), BF16)
    for b in range(blocks):
        s = slice(b * B, (b + 1) * B)
        length = u[b : b + 1, B - 1 :]
        value = inside[s, :] + dot(lanes[s, :], state_rows(state))
        excitation[s, :] = value
        product = value * xrows[s, :]
        high, low = split(product)
        total = lax.dot_general(ones, high, NT, preferred_element_type=F32)
        total = total + lax.dot_general(ones, low, NT, preferred_element_type=F32)
        partial[b : b + 1, :] = total[0:1, :] * (1.0 / rank)
        state = state * jnp.exp(-dw * length) + sums[b * count : (b + 1) * count, :]
    comp = jnp.zeros((8, width), F32)
    for b in reversed(range(blocks)):
        s = slice(b * B, (b + 1) * B)
        ub = u[b : b + 1, :]
        length = ub[:, B - 1 :]
        left = jnp.sum(w * (1.0 - jnp.exp(-d * (length - ub + after))), axis=0, keepdims=True)
        remain[b : b + 1, :] = left
        comp = comp + two_term(jnp.broadcast_to(left, (8, B)), srows[s, :].astype(BF16))
        after = after + length
    misc[0:8, :] = comp
    misc[8:16, :] = jnp.broadcast_to(end, (8, width))


def reverse_kernel(count, decay, u_ref, marks, base_e, total, xrows, comp, inverse, sums, device, base_sum):
    blocks = u_ref.shape[0]
    u = u_ref[...]
    inv = 1.0 / (base_e[...] + total[...])
    inverse[...] = inv
    width = xrows.shape[1]
    d, dw = down(decay, count), down(decay, count, width)
    groups = base_sum.shape[0]
    pending = jnp.zeros((count, width), F32)
    both = jnp.zeros((2 * groups, B), F32)
    for b in reversed(range(blocks)):
        s = slice(b * B, (b + 1) * B)
        ub = u[b : b + 1, :]
        length = ub[:, B - 1 :]
        ib = inv[b : b + 1, :]
        part = two_term(d * jnp.exp(-d * ub) * ib, xrows[s, :].astype(BF16))
        sums[b * count : (b + 1) * count, :] = part
        pending = pending * jnp.exp(-dw * length) + part
        m = marks[b : b + 1, :]
        hi, lo = m // B, lax.rem(m, B)
        ih = ib.astype(BF16).astype(F32)
        spread = jnp.concatenate([jnp.broadcast_to(ih, (groups, B)), jnp.broadcast_to(ib - ih, (groups, B))], 0)
        left = jnp.where(lax.rem(iota((2 * groups, B), 0), groups) == hi, spread, 0.0).astype(BF16)
        right = (iota((B, B), 0) == lo).astype(BF16)
        both = both + lax.dot_general(left, right, NT, preferred_element_type=F32)
    base_sum[...] = both[:groups] + both[groups:]
    device[0:count, :] = pending
    device[count:, :] = comp[0:8, :]


def scatter(marks, values, out):
    def group(g, _):
        e = g * 4
        m = [marks[e + j] for j in range(4)]
        add = [values[pl.ds(e + j, 1), :] for j in range(4)]
        old = [out[pl.ds(r, 1), :] for r in m]
        for j in range(4):
            new = old[j] + add[j]
            for i in range(j):
                new = new + jnp.where(m[i] == m[j], add[i], 0.0)
            out[pl.ds(m[j], 1), :] = new
        return 0

    lax.fori_loop(0, values.shape[0] // 4, group, 0, unroll=4)


def clear(out):
    def zero(i, _):
        out[pl.ds(pl.multiple_of(i * 8, 8), 8), :] = jnp.zeros((8, out.shape[1]), F32)
        return 0

    lax.fori_loop(0, out.shape[0] // 8, zero, 0, unroll=8)


def scatter_excite_kernel(marks, inverse, excitation, out, values):
    blocks = inverse.shape[0]
    clear(out)
    cols = columns(inverse[...])
    for b in range(blocks):
        s = slice(b * B, (b + 1) * B)
        values[s, :] = excitation[s, :] * cols[:, b : b + 1]
    scatter(marks, values, out)


def scatter_source_kernel(
    count, weights, decay, place, marks, u_ref, inverse, remain, misc, xtot, summaries, back, sums, sym, xrows,
    out, fin, values,
):
    blocks = u_ref.shape[0]
    peers = summaries.shape[0]
    me = place[0]
    clear(out)
    u = u_ref[...]
    width = xrows.shape[1]
    dw = down(decay, count, width)
    wide_d, wide_w = across(decay, count, 3), across(weights, count, 3)
    pending = jnp.zeros((count, width), F32)
    comp = jnp.zeros((1, width), F32)
    for r in reversed(range(peers)):
        length = summaries[r, count : count + 1, 0:1]
        pending = jnp.where(r > me, pending * jnp.exp(-dw * length) + back[r, 0:count, :], pending)
        comp = comp + back[r, count : count + 1, :]
    fin[0:8, :] = jnp.broadcast_to(comp, (8, width))
    fin[8:16, :] = misc[8:16, :]
    ut, rem_t = columns(u), columns(remain[...])
    share = xtot[0:1, :] * (1.0 / out.shape[0])
    later = iota((B, B), 0) < iota((B, B), 1)
    for b in reversed(range(blocks)):
        s = slice(b * B, (b + 1) * B)
        length = u[b : b + 1, B - 1 :]
        high, low = split(jnp.where(later, sym[s, :] * inverse[b : b + 1, :], 0.0))
        x = xrows[s, :].astype(BF16)
        lanes = state_lanes(wide_w * jnp.exp(-wide_d * (length - ut[:, b : b + 1])), count)
        value = dot(high, x) + dot(low, x) + dot(lanes, state_rows(pending))
        values[s, :] = value - rem_t[:, b : b + 1] * share
        pending = pending * jnp.exp(-dw * length) + sums[b * count : (b + 1) * count, :]
    scatter(marks, values, out)


def call(kernel, ins, outs, scratch=(), flops=10**8):
    return pl.pallas_call(
        kernel,
        out_shape=[jax.ShapeDtypeStruct(s, t) for s, t in outs],
        in_specs=list(ins),
        out_specs=[VMEM] * len(outs),
        scratch_shapes=list(scratch),
        compiler_params=pltpu.CompilerParams(vmem_limit_bytes=40 * 2**20),
        cost_estimate=pl.CostEstimate(flops=flops, bytes_accessed=4 * 2**20, transcendentals=10**6),
    )


def body(marks, gaps, excite, source, base_rate, weights, decay):
    events = marks.shape[0]
    blocks = events // B
    slices, types = excite.shape
    rank = slices * lax.axis_size("mark")
    peers = lax.axis_size("tm")
    count = decay.shape[0]
    place = lax.axis_index("tm").reshape(1)
    flat = marks.reshape(blocks, B)
    rows = ((events, slices), F32)
    plane = ((blocks, B), F32)
    parts = ((blocks * count, slices), F32)
    packet = ((count + 8, slices), F32)

    srows, xrows, u, sums, device, xtot = call(
        functools.partial(gather_kernel, count),
        [SMEM, SMEM, VMEM, VMEM, VMEM],
        [rows, rows, plane, parts, packet, ((8, slices), F32)],
        [pltpu.VMEM((types, slices), F32)] * 2,
    )(marks, decay, gaps.reshape(blocks, B), source, excite)
    summaries = lax.all_gather(device, "tm")
    sym, inside, lanes, base_e = call(
        functools.partial(inside_kernel, count),
        [SMEM, SMEM] + [VMEM] * 4,
        [((events, B), F32), rows, ((events, B), BF16), plane],
        flops=5 * 10**9,
    )(weights, decay, u, flat, base_rate.reshape(types // B, B), srows)
    excitation, partial, remain, misc = call(
        functools.partial(forward_kernel, count, rank),
        [SMEM, SMEM, SMEM] + [VMEM] * 7,
        [rows, plane, plane, ((16, slices), F32)],
    )(weights, decay, place, u, summaries, sums, lanes, inside, srows, xrows)
    total = lax.psum(partial, "mark")
    inverse, back_sums, back_device, base_sum = call(
        functools.partial(reverse_kernel, count),
        [SMEM] + [VMEM] * 6,
        [plane, parts, packet, ((types // B, B), F32)],
    )(decay, u, flat, base_e, total, xrows, misc)
    back = lax.all_gather(back_device, "tm")
    (excite_term,) = call(
        scatter_excite_kernel,
        [SMEM] + [VMEM] * 2,
        [((types, slices), F32)],
        [pltpu.VMEM((events, slices), F32)],
        flops=10**10,
    )(marks, inverse, excitation)
    base_part = lax.psum_scatter(base_sum.reshape(types), "tm", scatter_dimension=0, tiled=True)
    excite_part = lax.psum_scatter(excite_term, "tm", scatter_dimension=0, tiled=True)
    source_term, fin = call(
        functools.partial(scatter_source_kernel, count),
        [SMEM] * 4 + [VMEM] * 10,
        [((types, slices), F32), ((16, slices), F32)],
        [pltpu.VMEM((events, slices), F32)],
        flops=10**10,
    )(weights, decay, place, marks, u, inverse, remain, misc, xtot, summaries, back, back_sums, sym, xrows)
    source_part = lax.psum_scatter(source_term, "tm", scatter_dimension=0, tiled=True)

    events_all = events * peers
    factor = types / events_all
    grad_excite = factor * excite_part.T - fin[0][:, None] / events_all
    grad_base = factor * base_part - fin[8, 0] / events_all
    return grad_excite, factor * source_part.T, grad_base


def solution(mesh):
    return jax.shard_map(
        body,
        mesh=mesh,
        in_specs=(P("tm"), P("tm"), P("mark", None), P("mark", None), P(), P(), P()),
        out_specs=(P("mark", "tm"), P("mark", "tm"), P("tm")),
        check_vma=False,
    )
```

time: 518 us -> 292 us (0.56)
  other arithmetic: 112 us -> 2.75 us
  matrix products: 73.8 us -> 0 us
  local copies, waits for them, and re-layouts: 90.3 us -> 19.5 us
  blocking collectives: 53 us -> 112 us
  Pallas kernels: 0 us -> 54.8 us
  starting transfers between devices: 51.9 us -> 0.08 us
  loops' own time: 29.7 us -> 0 us
  between operations: 30.7 us -> 15.5 us
  waiting for transfers between devices: 75 us -> 87.1 us
    dot_general x53 -> x0, matrix products: 73.8 us -> none  [the longest x8 24 us: backward_block(): jnp.dot(kernel.T, weighted, precision=highest)]
    scatter-add x3 -> x0, other arithmetic: 71.6 us -> none  [the longest x1 24.8 us: body(): jax.ops.segment_sum(feedback - remainder[:, None] * excite_total[None, :]...]
    all_gather x0 -> x2, blocking collectives: none -> 63.4 us  [the longest x1 32.3 us: body(): summaries = lax.all_gather(device, 'tm')]
    reduce_scatter x2, waiting for transfers between devices: 24.8 us -> 87.1 us  [the longest x1 87.1 us: body(): lax.psum_scatter(source_term, 'tm', scatter_dimension=0, tiled=True)]
    pallas_call x0 -> x6, Pallas kernels: none -> 54.8 us  [the longest x1 16.3 us: body(): call(functools.partial(scatter_source_kernel, count), [SMEM] * 4 + [VMEM]...]
    ppermute x21 -> x0, starting transfers between devices: 51.6 us -> none  [passed_along(): return lax.ppermute(array, axis, pairs)]
    gather x4 -> x0, local copies, waits for them, and re-layouts: 51.4 us -> none  [the longest x1 23 us: body(): jnp.take(base_rate, event_marks) + lax.psum(partial_value, 'mark')]
    ppermute x21 -> x0, waiting for transfers between devices: 50.1 us -> none  [passed_along(): return lax.ppermute(array, axis, pairs)]
  transfers between devices with their start and end apart: 23 -> 2, of which waited for: 15 -> 1; matrix products, arithmetic and copies ran while one was open for 24% -> 1% of each run, Pallas kernels for 0% -> 6%
where the time goes in v1:
time: 292 us
  blocking collectives  112 us (38%)
  waiting for transfers between devices  87.1 us (30%)
  Pallas kernels  54.8 us (19%)
  local copies, waits for them, and re-layouts  19.5 us (7%)
  between operations  15.5 us (5%)
    reduce_scatter x1, waiting for transfers between devices, body(): lax.psum_scatter(source_term, 'tm', scatter_dimension=0, tiled=True)  87.1 us
    unnamed x1, blocking collectives  38.5 us
    all_gather x1, blocking collectives, body(): summaries = lax.all_gather(device, 'tm')  32.3 us
    all_gather x1, blocking collectives, body(): back = lax.all_gather(back_device, 'tm')  31.1 us
    unnamed x39, local copies, waits for them, and re-layouts  19 us
    pallas_call x1, Pallas kernels, body(): call(functools.partial(scatter_source_kernel, count), [SMEM] * 4 + [VMEM]...  16.3 us
    pallas_call x1, Pallas kernels, body(): call(functools.partial(gather_kernel, count), [SMEM, SMEM, VMEM, VMEM, VM...  14.1 us
    pallas_call x1, Pallas kernels, body(): call(scatter_excite_kernel, [SMEM] + [VMEM] * 2, [((types, slices), F32)]...  13.3 us
  transfers between devices with their start and end apart: 2, of which 1 were waited for; matrix products, arithmetic and copies ran while one was open for 1% of the time, Pallas kernels for 6%

profile of v1, /device:TPU:0, one launch (start us, length us, event | category | flops | bytes accessed | tf_op | source)
XLA Modules:
  0.0 291.8 jit_solution(6044808014777391128)
XLA Ops:
  7.2 1.6 copy-done.2
  8.8 1.6 copy-done.3
  12.5 14.1 %shard_map.94 = (f32[4096,128]{1,0:T(8,128)S(1)}, f32[4096,128]{1,0:T(8,128)S(1)}, f32[32,128]{1,0:T(8,128)S(1)}, f32[256,128]{1,0:T(8,128)S(1)}, f32[16,128]{1,0:T(8,128)S(1)}, /*index=5*/f32[8,128]{1,0:T(8,128)S(1)}) custom-call(s32[4096]{0:T(1024)S(1)} %copy-done.6, f32[8]{0:T(128)S(1)} %copy-done.9, s32[32,128]{1,0:T(8,128)S(1)} %bitcast.21, ...), custom_call_target="tpu_custom_call" | custom-call | flops 100000000 | bytes 4194304 | tf_op jit(solution)/shard_map/pallas_call | solution.py:318
  26.6 1.4 copy-done.4
  28.0 32.3 %all-gather = f32[128,128]{1,0:T(8,128)S(1)} all-gather(f32[16,128]{1,0:T(8,128)S(1)} %get-tuple-element.26), channel_id=2, replica_groups=mesh['tm'=8,'mark'=4] {'tm'}, dimensions={0}, use_global_device_ids=true | all-gather | bytes 73728 | tf_op jit(solution)/shard_map/all_gather | solution.py:324
  60.3 1.6 copy-done.5
  61.8 5.2 %shard_map.95 = (f32[4096,128]{1,0:T(8,128)S(1)}, f32[4096,128]{1,0:T(8,128)S(1)}, bf16[4096,128]{1,0:T(8,128)(2,1)S(1)}, f32[32,128]{1,0:T(8,128)S(1)}) custom-call(f32[8]{0:T(128)S(1)} %copy-done.11, f32[8]{0:T(128)S(1)} %copy-done.10, f32[32,128]{1,0:T(8,128)S(1)} %get-tuple-element.23.u_ref, s32[32,128]{1,0:T(8,128)S(1)} %bitcast.17, ...), custom_call_target="tpu_custom_call" | custom-call | flops 5000000000 | bytes 4194304 | tf_op jit(solution)/shard_map/pallas_call | solution.py:325
  67.1 1.3 copy-done.15
  68.4 4.2 %shard_map.96 = (f32[4096,128]{1,0:T(8,128)S(1)}, f32[32,128]{1,0:T(8,128)S(1)}, f32[32,128]{1,0:T(8,128)S(1)}, f32[16,128]{1,0:T(8,128)S(1)}) custom-call(f32[8]{0:T(128)S(1)} %copy-done.11, f32[8]{0:T(128)S(1)} %copy-done.10, s32[1]{0:T(128)} %bitcast.3.place, f32[32,128]{1,0:T(8,128)S(1)} %get-tuple-element.23.u_ref, f32[8,16,128]{2,1,0:T(8,128)S(1)} %bitcast.15, ...), custom_call_target="tpu_custom_call" | custom-call | flops 100000000 | bytes 4194304 | tf_op jit(solution)/shard_map/pallas_call | solution.py:331
  72.6 1.4 copy-done.12
  74.0 10.1 %psum.7.total = f32[32,128]{1,0:T(8,128)S(1)} all-reduce(f32[32,128]{1,0:T(8,128)S(1)} %get-tuple-element.31), channel_id=1, replica_groups=mesh['tm'=8,'mark'=4] {'mark'}, use_global_device_ids=true, to_apply=%region_0.0 | all-reduce | flops 4096 | bytes 32768 | tf_op jit(solution)/shard_map/psum | solution.py:336
  84.1 1.7 shard_map.97
  85.8 13.3 %shard_map.98 = f32[8192,128]{1,0:T(8,128)S(1)} custom-call(s32[4096]{0:T(1024)S(1)} %copy-done.7, f32[32,128]{1,0:T(8,128)S(1)} %get-tuple-element.33.inverse, f32[4096,128]{1,0:T(8,128)S(1)} %copy-done.13), custom_call_target="tpu_custom_call" | custom-call | flops 10000000000 | bytes 4194304 | tf_op jit(solution)/shard_map/pallas_call | solution.py:343
  99.1 2.0 copy-done
  101.1 31.1 %all-gather.1 = f32[128,128]{1,0:T(8,128)S(1)} all-gather(f32[16,128]{1,0:T(8,128)S(1)} %get-tuple-element.37), channel_id=3, replica_groups=mesh['tm'=8,'mark'=4] {'tm'}, dimensions={0}, use_global_device_ids=true | all-gather | bytes 73728 | tf_op jit(solution)/shard_map/all_gather | solution.py:342
  132.2 1.6 copy-done.16
  133.8 16.3 %shard_map.99 = (f32[8192,128]{1,0:T(8,128)S(1)}, f32[16,128]{1,0:T(8,128)S(1)}) custom-call(f32[8]{0:T(128)S(1)} %copy-done.11, f32[8]{0:T(128)S(1)} %copy-done.10, s32[1]{0:T(128)} %bitcast.3.place, s32[4096]{0:T(1024)S(1)} %copy-done.7, f32[32,128]{1,0:T(8,128)S(1)} %get-tuple-element.23.u_ref, f32[32,128]{1,0:T(8,128)S(1)} %get-tuple-element.33.inverse, ...), custom_call_target="tpu_custom_call" | custom-call | flops 10000000000 | bytes 4194304 | tf_op jit(solution)/shard_map/pallas_call | solution.py:352
  150.2 2.0 copy-done.1
  154.6 38.5 %all-reduce = f32[8192]{0:T(1024)S(1)} all-reduce(f32[8192]{0:T(1024)S(1)} %bitcast.20), channel_id=6, replica_groups=mesh['tm'=8,'mark'=4] {'tm'}, use_global_device_ids=true, to_apply=%region_3.0.clone | all-reduce | flops 8192 | bytes 65536
  193.7 1.1 subtract_bitcast_fusion
  194.8 1.0 copy.12
  195.8 87.1 %reduce-scatter.5.cloned.1.call-done = f32[1024,128]{1,0:T(8,128)} async-done(((f32[8192,128]{1,0:T(8,128)}), f32[1024,128]{1,0:T(8,128)}) %reduce-scatter.5.cloned.1.call-update) | async-done | bytes 524304 | tf_op jit(solution)/shard_map/reduce_scatter | solution.py:359
  282.9 1.1 multiply_bitcast_fusion
  284.0 1.0 copy.13
  (36 shorter events, 3.9 us)
Async XLA Ops:
  7.2 186.6 %reduce-scatter.3.cloned.1.call-start = ((), (), s32[]{:S(2)}) async-start(), calls=%async_computation.2 | async-start | bytes 4718592 | tf_op jit(solution)/shard_map/reduce_scatter | solution.py:351
  7.2 1.6 copy-start.2
  8.8 1.6 copy-start.3
  10.4 0.7 copy-start.6
  11.1 0.7 copy-start.8
  11.8 0.7 copy-start.9
  12.5 47.7 %copy-start.7 = (s32[4096]{0:T(1024)S(1)}, s32[4096]{0:T(1024)}, u32[]{:S(2)}) copy-start(s32[4096]{0:T(1024)} %marks.5) | copy-start | bytes 49156
  12.5 47.7 %copy-start.10 = (f32[8]{0:T(128)S(1)}, f32[8]{0:T(128)}, u32[]{:S(2)}) copy-start(f32[8]{0:T(128)} %decay.9) | copy-start | bytes 100
  12.5 47.7 %copy-start.11 = (f32[8]{0:T(128)S(1)}, f32[8]{0:T(128)}, u32[]{:S(2)}) copy-start(f32[8]{0:T(128)} %weights.5) | copy-start | bytes 100
  12.5 47.7 %copy-start.14 = (f32[8192]{0:T(1024)S(1)}, f32[8192]{0:T(1024)}, u32[]{:S(2)}) copy-start(f32[8192]{0:T(1024)} %param.11) | copy-start | bytes 98308
  26.6 1.4 copy-start.4
  60.2 1.6 copy-start.5
  67.1 1.4 copy-start.15
  72.6 1.4 copy-start.12
  84.1 1.7 copy-start.13
  99.0 2.0 copy-start
  101.0 181.8 %reduce-scatter.5.cloned.1.call-start = ((), (), s32[]{:S(2)}) async-start(), calls=%async_computation.3 | async-start | bytes 4718592 | tf_op jit(solution)/shard_map/reduce_scatter | solution.py:359
  132.2 1.6 copy-start.16
  150.2 2.0 copy-start.1
  152.1 1.2 copy-start.17
Sparse Core Ops, SparseCore 0:
  101.2 89.6 reduce-scatter.2
  194.9 87.8 reduce-scatter.4

commit v2 on v1

--- a/solution.py
+++ b/solution.py
@@ -193,7 +193,7 @@
 def reverse_kernel(count, decay, u_ref, marks, base_e, total, xrows, comp, inverse, sums, device, base_sum):
     blocks = u_ref.shape[0]
     u = u_ref[...]
-    inv = 1.0 / (base_e[...] + total[...])
+    inv = 1.0 / (base_e[...] + sum(total[r] for r in range(total.shape[0])))
     inverse[...] = inv
     width = xrows.shape[1]
     d, dw = down(decay, count), down(decay, count, width)
@@ -301,6 +301,127 @@
     )
 
 
+def exchange_kernel(axis, n, spread, *refs):
+    k = len(spread)
+    ins, outs, send, recv = refs[:k], refs[k : 2 * k], refs[2 * k], refs[2 * k + 1]
+    me = lax.axis_index(axis)
+    peers = [lax.rem(me + i, n) for i in range(1, n)]
+    barrier = pltpu.get_barrier_semaphore()
+    for p in peers:
+        pl.semaphore_signal(barrier, inc=1, device_id={axis: p}, device_id_type=pl.DeviceIdType.MESH)
+    pl.semaphore_wait(barrier, n - 1)
+    copies = []
+    for a in range(k):
+        for i, p in enumerate(peers):
+            copy = pltpu.make_async_remote_copy(
+                src_ref=ins[a].at[p] if spread[a] else ins[a],
+                dst_ref=outs[a].at[me],
+                send_sem=send.at[a, i],
+                recv_sem=recv.at[a, i],
+                device_id={axis: p},
+                device_id_type=pl.DeviceIdType.MESH,
+            )
+            copy.start()
+            copies.append(copy)
+    for a in range(k):
+        outs[a][me] = ins[a][me] if spread[a] else ins[a][...]
+    for copy in copies:
+        copy.wait()
+
+
+def exchange(arrays, axis, spread, collective):
+    n = lax.axis_size(axis)
+    k = len(arrays)
+    shapes = [a.shape if s else (n,) + a.shape for a, s in zip(arrays, spread)]
+    return pl.pallas_call(
+        functools.partial(exchange_kernel, axis, n, spread),
+        out_shape=[jax.ShapeDtypeStruct(s, F32) for s in shapes],
+        in_specs=[VMEM] * k,
+        out_specs=[VMEM] * k,
+        scratch_shapes=[pltpu.SemaphoreType.DMA((k, n - 1))] * 2,
+        compiler_params=pltpu.CompilerParams(collective_id=collective, has_side_effects=True),
+    )(*arrays)
+
+
+def ring_kernel(n, x0, x1, out0, out1, slots, send, recv):
+    xs, outs = (x0, x1), (out0, out1)
+    per = out0.shape[0]
+    half = per // 2
+    me = lax.axis_index("tm")
+    odd = lax.rem(me, 2)
+    at = lax.div(me, 2) + odd * (lax.div(2 * n - 1 - me, 2) - lax.div(me, 2))
+
+    def member(place):
+        c = lax.rem(place + 2 * n, n)
+        return 2 * c + lax.div(c, n // 2) * (2 * n - 1 - 4 * c)
+
+    towards = (member(at + 1), member(at - 1))
+    barrier = pltpu.get_barrier_semaphore()
+    for p in towards:
+        pl.semaphore_signal(barrier, inc=1, device_id={"tm": p}, device_id_type=pl.DeviceIdType.MESH)
+    pl.semaphore_wait(barrier, 2)
+
+    def rows(j, step):
+        way = j % 2
+        block = member(at + 1 + step) if way else member(at - 1 - step)
+        return pl.ds(pl.multiple_of(block * per + way * half, 8), half)
+
+    def copy(j, step, source):
+        return pltpu.make_async_remote_copy(
+            src_ref=source,
+            dst_ref=slots.at[j, step],
+            send_sem=send.at[j, step],
+            recv_sem=recv.at[j, step],
+            device_id={"tm": towards[j % 2]},
+            device_id_type=pl.DeviceIdType.MESH,
+        )
+
+    for j in range(4):
+        copy(j, 0, xs[j // 2].at[rows(j, 0)]).start()
+
+    def step(s, _):
+        for j in range(4):
+            held = slots.at[j, s - 1]
+            copy(j, s - 1, held).wait_recv()
+            held[...] += xs[j // 2][rows(j, s), :]
+            copy(j, s, held).start()
+        return 0
+
+    lax.fori_loop(1, n - 1, step, 0)
+    for j in range(4):
+        copy(j, n - 2, slots.at[j, n - 2]).wait_recv()
+        start = (j % 2) * half
+        own = pl.ds(pl.multiple_of(me * per + start, 8), half)
+        outs[j // 2][start : start + half, :] = slots[j, n - 2] + xs[j // 2][own, :]
+
+    def sent(s, _):
+        for j in range(4):
+            copy(j, s, slots.at[j, s]).wait_send()
+        return 0
+
+    lax.fori_loop(0, n - 1, sent, 0)
+
+
+def ring_sum(x0, x1):
+    n = lax.axis_size("tm")
+    types, width = x0.shape
+    per = types // n
+    return pl.pallas_call(
+        functools.partial(ring_kernel, n),
+        out_shape=[jax.ShapeDtypeStruct((per, width), F32)] * 2,
+        in_specs=[VMEM] * 2,
+        out_specs=[VMEM] * 2,
+        scratch_shapes=[
+            pltpu.VMEM((4, n - 1, per // 2, width), F32),
+            pltpu.SemaphoreType.DMA((4, n - 1)),
+            pltpu.SemaphoreType.DMA((4, n - 1)),
+        ],
+        compiler_params=pltpu.CompilerParams(
+            collective_id=3, has_side_effects=True, vmem_limit_bytes=40 * 2**20
+        ),
+    )(x0, x1)
+
+
 def body(marks, gaps, excite, source, base_rate, weights, decay):
     events = marks.shape[0]
     blocks = events // B
@@ -321,7 +442,7 @@
         [rows, rows, plane, parts, packet, ((8, slices), F32)],
         [pltpu.VMEM((types, slices), F32)] * 2,
     )(marks, decay, gaps.reshape(blocks, B), source, excite)
-    summaries = lax.all_gather(device, "tm")
+    (summaries,) = exchange([device], "tm", [False], 0)
     sym, inside, lanes, base_e = call(
         functools.partial(inside_kernel, count),
         [SMEM, SMEM] + [VMEM] * 4,
@@ -333,13 +454,15 @@
         [SMEM, SMEM, SMEM] + [VMEM] * 7,
         [rows, plane, plane, ((16, slices), F32)],
     )(weights, decay, place, u, summaries, sums, lanes, inside, srows, xrows)
-    total = lax.psum(partial, "mark")
+    (total,) = exchange([partial], "mark", [False], 1)
     inverse, back_sums, back_device, base_sum = call(
         functools.partial(reverse_kernel, count),
         [SMEM] + [VMEM] * 6,
         [plane, parts, packet, ((types // B, B), F32)],
     )(decay, u, flat, base_e, total, xrows, misc)
-    back = lax.all_gather(back_device, "tm")
+    back, base_parts = exchange(
+        [back_device, base_sum.reshape(peers, types // B // peers, B)], "tm", [False, True], 2
+    )
     (excite_term,) = call(
         scatter_excite_kernel,
         [SMEM] + [VMEM] * 2,
@@ -347,8 +470,6 @@
         [pltpu.VMEM((events, slices), F32)],
         flops=10**10,
     )(marks, inverse, excitation)
-    base_part = lax.psum_scatter(base_sum.reshape(types), "tm", scatter_dimension=0, tiled=True)
-    excite_part = lax.psum_scatter(excite_term, "tm", scatter_dimension=0, tiled=True)
     source_term, fin = call(
         functools.partial(scatter_source_kernel, count),
         [SMEM] * 4 + [VMEM] * 10,
@@ -356,7 +477,8 @@
         [pltpu.VMEM((events, slices), F32)],
         flops=10**10,
     )(weights, decay, place, marks, u, inverse, remain, misc, xtot, summaries, back, back_sums, sym, xrows)
-    source_part = lax.psum_scatter(source_term, "tm", scatter_dimension=0, tiled=True)
+    excite_part, source_part = ring_sum(excite_term, source_term)
+    base_part = jnp.sum(base_parts, axis=0).reshape(types // peers)
 
     events_all = events * peers
     factor = types / events_all

time: 292 us -> 185 us (0.63)
  blocking collectives: 112 us -> 0 us
  Pallas kernels: 54.8 us -> 161 us
  waiting for transfers between devices: 87.1 us -> 0 us
  between operations: 15.5 us -> 1.52 us
    pallas_call x0 -> x4, Pallas kernels: none -> 106 us  [the longest x1 81.6 us: ring_sum(): pl.pallas_call(functools.partial(ring_kernel, n), out_shape=[jax.ShapeDty...]
    reduce_scatter x2 -> x0, waiting for transfers between devices: 87.1 us -> none  [the longest x1 87.1 us: body(): lax.psum_scatter(source_term, 'tm', scatter_dimension=0, tiled=True)]
    all_gather x2 -> x0, blocking collectives: 63.4 us -> none  [the longest x1 32.3 us: body(): summaries = lax.all_gather(device, 'tm')]
    unnamed x1 -> x0, blocking collectives: 38.5 us -> none
    psum x1 -> x0, blocking collectives: 10.1 us -> none  [body(): total = lax.psum(partial, 'mark')]
    unnamed x39 -> x52, local copies, waits for them, and re-layouts: 19 us -> 20.8 us
  transfers between devices with their start and end apart: 2 -> 0, of which waited for: 1 -> 0; matrix products, arithmetic and copies ran while one was open for 1% -> 0% of each run, Pallas kernels for 6% -> 0%
where the time goes in v2:
time: 185 us; the launch traced here: 184 us
  Pallas kernels  161 us (87%)
  local copies, waits for them, and re-layouts  21.3 us (12%)
    pallas_call x1, Pallas kernels, ring_sum(): pl.pallas_call(functools.partial(ring_kernel, n), out_shape=[jax.ShapeDty...  81.6 us
    pallas_call x3, Pallas kernels, exchange(): pl.pallas_call(functools.partial(exchange_kernel, axis, n, spread), out_s...  24.2 us
    unnamed x52, local copies, waits for them, and re-layouts  20.8 us
    pallas_call x1, Pallas kernels, body(): call(functools.partial(scatter_source_kernel, count), [SMEM] * 4 + [VMEM]...  16.3 us
    pallas_call x1, Pallas kernels, body(): call(functools.partial(gather_kernel, count), [SMEM, SMEM, VMEM, VMEM, VM...  14.1 us
    pallas_call x1, Pallas kernels, body(): call(scatter_excite_kernel, [SMEM] + [VMEM] * 2, [((types, slices), F32)]...  13.3 us
    pallas_call x1, Pallas kernels, body(): call(functools.partial(inside_kernel, count), [SMEM, SMEM] + [VMEM] * 4,...  5.3 us
    pallas_call x1, Pallas kernels, body(): call(functools.partial(forward_kernel, count, rank), [SMEM, SMEM, SMEM] +...  4.22 us

profile of v2, /device:TPU:0, one launch (start us, length us, event | category | flops | bytes accessed | tf_op | source)
XLA Modules:
  0.0 184.2 jit_solution(4446884758952007433)
XLA Ops:
  0.6 1.6 copy-done.2
  2.2 1.6 copy-done.3
  3.8 0.7 copy-done.8
  4.5 0.7 copy-done.11
  5.9 14.1 %shard_map.94 = (f32[4096,128]{1,0:T(8,128)S(1)}, f32[4096,128]{1,0:T(8,128)S(1)}, f32[32,128]{1,0:T(8,128)S(1)}, f32[256,128]{1,0:T(8,128)S(1)}, f32[16,128]{1,0:T(8,128)S(1)}, /*index=5*/f32[8,128]{1,0:T(8,128)S(1)}) custom-call(s32[4096]{0:T(1024)S(1)} %copy-done.8, f32[8]{0:T(128)S(1)} %copy-done.15, s32[32,128]{1,0:T(8,128)S(1)} %bitcast.17, ...), custom_call_target="tpu_custom_call" | custom-call | flops 100000000 | bytes 4194304 | tf_op jit(solution)/shard_map/pallas_call | solution.py:439
  20.0 1.4 copy-done.4
  22.0 10.0 %shard_map.96.summaries = f32[8,16,128]{2,1,0:T(8,128)} custom-call(f32[16,128]{1,0:T(8,128)} %copy-done.14), custom_call_target="tpu_custom_call" | custom-call | tf_op jit(solution)/shard_map/pallas_call | solution.py:336
  32.0 1.6 copy-done.5
  33.6 5.3 %shard_map.95 = (f32[4096,128]{1,0:T(8,128)S(1)}, f32[4096,128]{1,0:T(8,128)S(1)}, bf16[4096,128]{1,0:T(8,128)(2,1)S(1)}, f32[32,128]{1,0:T(8,128)S(1)}) custom-call(f32[8]{0:T(128)S(1)} %copy-done.17, f32[8]{0:T(128)S(1)} %copy-done.16, f32[32,128]{1,0:T(8,128)S(1)} %get-tuple-element.27.u_ref, s32[32,128]{1,0:T(8,128)S(1)} %bitcast.14, ...), custom_call_target="tpu_custom_call" | custom-call | flops 5000000000 | bytes 4194304 | tf_op jit(solution)/shard_map/pallas_call | solution.py:446
  38.9 4.2 %shard_map.97 = (f32[4096,128]{1,0:T(8,128)S(1)}, f32[32,128]{1,0:T(8,128)S(1)}, f32[32,128]{1,0:T(8,128)S(1)}, f32[16,128]{1,0:T(8,128)S(1)}) custom-call(f32[8]{0:T(128)S(1)} %copy-done.17, f32[8]{0:T(128)S(1)} %copy-done.16, s32[1]{0:T(128)} %bitcast.3.place, f32[32,128]{1,0:T(8,128)S(1)} %get-tuple-element.27.u_ref, f32[8,16,128]{2,1,0:T(8,128)S(1)} %copy-done.6, ...), custom_call_target="tpu_custom_call" | custom-call | flops 100000000 | bytes 4194304 | tf_op jit(solution)/shard_map/pallas_call | solution.py:452
  43.8 1.4 copy-done.18
  45.1 5.1 %shard_map.98.total = f32[4,32,128]{2,1,0:T(8,128)} custom-call(f32[32,128]{1,0:T(8,128)} %copy-done.12), custom_call_target="tpu_custom_call" | custom-call | tf_op jit(solution)/shard_map/pallas_call | solution.py:336
  50.3 0.8 copy-done.7
  51.1 1.7 shard_map.99
  54.0 9.1 %shard_map.101 = (f32[8,16,128]{2,1,0:T(8,128)}, f32[8,8,128]{2,1,0:T(8,128)}) custom-call(f32[16,128]{1,0:T(8,128)} %copy-done.13, f32[8,8,128]{2,1,0:T(8,128)} %bitcast.16), custom_call_target="tpu_custom_call" | custom-call | tf_op jit(solution)/shard_map/pallas_call | solution.py:336
  63.1 0.8 copy-done.20
  64.0 1.6 copy-done.23
  65.6 16.3 %shard_map.102 = (f32[8192,128]{1,0:T(8,128)S(1)}, f32[16,128]{1,0:T(8,128)S(1)}) custom-call(f32[8]{0:T(128)S(1)} %copy-done.17, f32[8]{0:T(128)S(1)} %copy-done.16, s32[1]{0:T(128)} %bitcast.3.place, s32[4096]{0:T(1024)S(1)} %copy-done.9, f32[32,128]{1,0:T(8,128)S(1)} %get-tuple-element.27.u_ref, f32[32,128]{1,0:T(8,128)S(1)} %get-tuple-element.37.inverse, ...), custom_call_target="tpu_custom_call" | custom-call | flops 10000000000 | bytes 4194304 | tf_op jit(solution)/shard_map/pallas_call | solution.py:473
  81.9 1.9 %copy-done = f32[8192,128]{1,0:T(8,128)} copy-done((f32[8192,128]{1,0:T(8,128)}, f32[8192,128]{1,0:T(8,128)S(1)}, u32[]{:S(2)}) %copy-start) | copy-done | bytes 4194328
  85.6 1.6 copy-done.19
  87.2 13.3 %shard_map.100.x0 = f32[8192,128]{1,0:T(8,128)S(1)} custom-call(s32[4096]{0:T(1024)S(1)} %copy-done.9, f32[32,128]{1,0:T(8,128)S(1)} %get-tuple-element.37.inverse, f32[4096,128]{1,0:T(8,128)S(1)} %copy-done.19), custom_call_target="tpu_custom_call" | custom-call | flops 10000000000 | bytes 4194304 | tf_op jit(solution)/shard_map/pallas_call | solution.py:466
  100.5 81.6 %shard_map.103 = (f32[1024,128]{1,0:T(8,128)S(1)}, f32[1024,128]{1,0:T(8,128)S(1)}) custom-call(f32[8192,128]{1,0:T(8,128)S(1)} %shard_map.100.x0, f32[8192,128]{1,0:T(8,128)S(1)} %copy-done.1), custom_call_target="tpu_custom_call" | custom-call | tf_op jit(solution)/shard_map/pallas_call | solution.py:409
  182.2 1.0 copy.11
  183.2 1.0 copy.10
  (43 shorter events, 4.3 us)
Async XLA Ops:
  0.6 1.6 copy-start.2
  2.2 1.6 copy-start.3
  3.8 0.7 copy-start.8
  4.5 0.7 copy-start.11
  5.3 0.7 copy-start.15
  5.9 26.1 %copy-start.9 = (s32[4096]{0:T(1024)S(1)}, s32[4096]{0:T(1024)}, u32[]{:S(2)}) copy-start(s32[4096]{0:T(1024)} %marks.5) | copy-start | bytes 49156
  5.9 26.1 %copy-start.16 = (f32[8]{0:T(128)S(1)}, f32[8]{0:T(128)}, u32[]{:S(2)}) copy-start(f32[8]{0:T(128)} %decay.9) | copy-start | bytes 100
  5.9 26.1 %copy-start.17 = (f32[8]{0:T(128)S(1)}, f32[8]{0:T(128)}, u32[]{:S(2)}) copy-start(f32[8]{0:T(128)} %weights.5) | copy-start | bytes 100
  5.9 26.1 %copy-start.21 = (f32[8192]{0:T(1024)S(1)}, f32[8192]{0:T(1024)}, u32[]{:S(2)}) copy-start(f32[8192]{0:T(1024)} %param.11) | copy-start | bytes 98308
  20.0 1.4 copy-start.4
  21.4 0.6 copy-start.14
  32.0 1.6 copy-start.5
  33.6 5.3 %copy-start.6 = (f32[8,16,128]{2,1,0:T(8,128)S(1)}, f32[8,16,128]{2,1,0:T(8,128)}, u32[]{:S(2)}) copy-start(f32[8,16,128]{2,1,0:T(8,128)} %shard_map.96.summaries) | copy-start | bytes 196612
  38.9 4.2 %copy-start.22 = (f32[4096,128]{1,0:T(8,128)}, f32[4096,128]{1,0:T(8,128)S(1)}, u32[]{:S(2)}) copy-start(f32[4096,128]{1,0:T(8,128)S(1)} %get-tuple-element.45.sym) | copy-start | bytes 6291460
  43.2 0.6 copy-start.12
  43.8 1.4 copy-start.18
  50.3 0.8 copy-start.7
  52.8 0.6 copy-start.10
  63.1 0.8 copy-start.20
  64.0 1.6 copy-start.23
  65.6 19.5 %copy-start.24 = (f32[8,8,128]{2,1,0:T(8,128)S(1)}, f32[8,8,128]{2,1,0:T(8,128)}, u32[]{:S(2)}) copy-start(f32[8,8,128]{2,1,0:T(8,128)} %get-tuple-element.50) | copy-start | bytes 98308
  81.9 2.0 %copy-start = (f32[8192,128]{1,0:T(8,128)}, f32[8192,128]{1,0:T(8,128)S(1)}, u32[]{:S(2)}) copy-start(f32[8192,128]{1,0:T(8,128)S(1)} %get-tuple-element.46.x1) | copy-start | bytes 12582916
  85.6 1.6 copy-start.19
  87.2 13.3 %copy-start.1 = (f32[8192,128]{1,0:T(8,128)S(1)}, f32[8192,128]{1,0:T(8,128)}, u32[]{:S(2)}) copy-start(f32[8192,128]{1,0:T(8,128)} %copy-done) | copy-start | bytes 12582916
  (1 other events, 0.6 us)

commit v3 on v2

--- a/solution.py
+++ b/solution.py
@@ -254,41 +254,6 @@
     scatter(marks, values, out)
 
 
-def scatter_source_kernel(
-    count, weights, decay, place, marks, u_ref, inverse, remain, misc, xtot, summaries, back, sums, sym, xrows,
-    out, fin, values,
-):
-    blocks = u_ref.shape[0]
-    peers = summaries.shape[0]
-    me = place[0]
-    clear(out)
-    u = u_ref[...]
-    width = xrows.shape[1]
-    dw = down(decay, count, width)
-    wide_d, wide_w = across(decay, count, 3), across(weights, count, 3)
-    pending = jnp.zeros((count, width), F32)
-    comp = jnp.zeros((1, width), F32)
-    for r in reversed(range(peers)):
-        length = summaries[r, count : count + 1, 0:1]
-        pending = jnp.where(r > me, pending * jnp.exp(-dw * length) + back[r, 0:count, :], pending)
-        comp = comp + back[r, count : count + 1, :]
-    fin[0:8, :] = jnp.broadcast_to(comp, (8, width))
-    fin[8:16, :] = misc[8:16, :]
-    ut, rem_t = columns(u), columns(remain[...])
-    share = xtot[0:1, :] * (1.0 / out.shape[0])
-    later = iota((B, B), 0) < iota((B, B), 1)
-    for b in reversed(range(blocks)):
-        s = slice(b * B, (b + 1) * B)
-        length = u[b : b + 1, B - 1 :]
-        high, low = split(jnp.where(later, sym[s, :] * inverse[b : b + 1, :], 0.0))
-        x = xrows[s, :].astype(BF16)
-        lanes = state_lanes(wide_w * jnp.exp(-wide_d * (length - ut[:, b : b + 1])), count)
-        value = dot(high, x) + dot(low, x) + dot(lanes, state_rows(pending))
-        values[s, :] = value - rem_t[:, b : b + 1] * share
-        pending = pending * jnp.exp(-dw * length) + sums[b * count : (b + 1) * count, :]
-    scatter(marks, values, out)
-
-
 def call(kernel, ins, outs, scratch=(), flops=10**8):
     return pl.pallas_call(
         kernel,
@@ -343,10 +308,41 @@
     )(*arrays)
 
 
-def ring_kernel(n, x0, x1, out0, out1, slots, send, recv):
+def feedback_values(count, me, weights, decay, u_ref, inverse, remain, xtot, summaries, back, sums, sym, xrows, types, pair):
+    blocks = u_ref.shape[0]
+    peers = summaries.shape[0]
+    u = u_ref[...]
+    width = xrows.shape[1]
+    dw = down(decay, count, width)
+    wide_d, wide_w = across(decay, count, 3), across(weights, count, 3)
+    pending = jnp.zeros((count, width), F32)
+    for r in reversed(range(peers)):
+        length = summaries[r, count : count + 1, 0:1]
+        pending = jnp.where(r > me, pending * jnp.exp(-dw * length) + back[r, 0:count, :], pending)
+    ut, rem_t = columns(u), columns(remain[...])
+    share = xtot[0:1, :] * (1.0 / types)
+    later = iota((B, B), 0) < iota((B, B), 1)
+    for b in reversed(range(blocks)):
+        s = slice(b * B, (b + 1) * B)
+        length = u[b : b + 1, B - 1 :]
+        high, low = split(jnp.where(later, sym[s, :] * inverse[b : b + 1, :], 0.0))
+        x = xrows[s, :].astype(BF16)
+        lanes = state_lanes(wide_w * jnp.exp(-wide_d * (length - ut[:, b : b + 1])), count)
+        value = dot(high, x) + dot(low, x) + dot(lanes, state_rows(pending))
+        value = value - rem_t[:, b : b + 1] * share
+        high, low = split(value)
+        pair[s, :] = jnp.concatenate([high.astype(F32), low.astype(F32)], 1).astype(BF16)
+        pending = pending * jnp.exp(-dw * length) + sums[b * count : (b + 1) * count, :]
+
+
+def ring_kernel(
+    n, count, weights, decay, x0, marks, u_ref, inverse, remain, xtot, summaries, back, sums, sym, xrows,
+    out0, out1, x1, pair, hot, slots, send, recv,
+):
     xs, outs = (x0, x1), (out0, out1)
-    per = out0.shape[0]
+    per, width = out0.shape
     half = per // 2
+    tile = hot.shape[0]
     me = lax.axis_index("tm")
     odd = lax.rem(me, 2)
     at = lax.div(me, 2) + odd * (lax.div(2 * n - 1 - me, 2) - lax.div(me, 2))
@@ -376,23 +372,64 @@
             device_id_type=pl.DeviceIdType.MESH,
         )
 
-    for j in range(4):
-        copy(j, 0, xs[j // 2].at[rows(j, 0)]).start()
-
-    def step(s, _):
-        for j in range(4):
+    def begin(chains):
+        for j in chains:
+            copy(j, 0, xs[j // 2].at[rows(j, 0)]).start()
+
+    def step(s, chains):
+        for j in chains:
             held = slots.at[j, s - 1]
             copy(j, s - 1, held).wait_recv()
             held[...] += xs[j // 2][rows(j, s), :]
             copy(j, s, held).start()
-        return 0
-
-    lax.fori_loop(1, n - 1, step, 0)
-    for j in range(4):
-        copy(j, n - 2, slots.at[j, n - 2]).wait_recv()
-        start = (j % 2) * half
-        own = pl.ds(pl.multiple_of(me * per + start, 8), half)
-        outs[j // 2][start : start + half, :] = slots[j, n - 2] + xs[j // 2][own, :]
+
+    def finish(chains):
+        for j in chains:
+            copy(j, n - 2, slots.at[j, n - 2]).wait_recv()
+            start = (j % 2) * half
+            own = pl.ds(pl.multiple_of(me * per + start, 8), half)
+            outs[j // 2][start : start + half, :] = slots[j, n - 2] + xs[j // 2][own, :]
+
+    def chunk(block):
+        def part(t, _):
+            first = block * per + t * tile
+            kind = iota((tile, B), 0) + first
+            for b in range(marks.shape[0]):
+                hot[:, b * B : (b + 1) * B] = (kind == marks[b : b + 1, :]).astype(BF16)
+            both = dot(hot[...], pair[...])
+            x1[pl.ds(pl.multiple_of(first, 8), tile), :] = both[:, :width] + both[:, width:]
+            return 0
+
+        lax.fori_loop(0, per // tile, part, 0)
+
+    begin((0, 1))
+    feedback_values(
+        count, me, weights, decay, u_ref, inverse, remain, xtot, summaries, back, sums, sym, xrows, x0.shape[0], pair
+    )
+
+    def excite_step(s, _):
+        step(s, (0, 1))
+        i = s - 1
+        away = lax.div(i, 2) + 1
+        chunk(member(at + away * (2 * lax.rem(i, 2) - 1)))
+        return 0
+
+    lax.fori_loop(1, n - 1, excite_step, 0)
+    begin((2, 3))
+
+    def rest(i, _):
+        chunk(member(at + i * (n // 2)))
+        return 0
+
+    lax.fori_loop(0, 2, rest, 0)
+    finish((0, 1))
+
+    def source_step(s, _):
+        step(s, (2, 3))
+        return 0
+
+    lax.fori_loop(1, n - 1, source_step, 0)
+    finish((2, 3))
 
     def sent(s, _):
         for j in range(4):
@@ -402,24 +439,28 @@
     lax.fori_loop(0, n - 1, sent, 0)
 
 
-def ring_sum(x0, x1):
+def ring_sum(count, weights, decay, x0, *rest):
     n = lax.axis_size("tm")
     types, width = x0.shape
     per = types // n
+    events = rest[-1].shape[0]
     return pl.pallas_call(
-        functools.partial(ring_kernel, n),
+        functools.partial(ring_kernel, n, count),
         out_shape=[jax.ShapeDtypeStruct((per, width), F32)] * 2,
-        in_specs=[VMEM] * 2,
+        in_specs=[SMEM] * 2 + [VMEM] * (1 + len(rest)),
         out_specs=[VMEM] * 2,
         scratch_shapes=[
+            pltpu.VMEM((types, width), F32),
+            pltpu.VMEM((events, 2 * width), BF16),
+            pltpu.VMEM((min(256, per), events), BF16),
             pltpu.VMEM((4, n - 1, per // 2, width), F32),
             pltpu.SemaphoreType.DMA((4, n - 1)),
             pltpu.SemaphoreType.DMA((4, n - 1)),
         ],
         compiler_params=pltpu.CompilerParams(
-            collective_id=3, has_side_effects=True, vmem_limit_bytes=40 * 2**20
+            collective_id=3, has_side_effects=True, vmem_limit_bytes=48 * 2**20
         ),
-    )(x0, x1)
+    )(weights, decay, x0, *rest)
 
 
 def body(marks, gaps, excite, source, base_rate, weights, decay):
@@ -470,20 +511,16 @@
         [pltpu.VMEM((events, slices), F32)],
         flops=10**10,
     )(marks, inverse, excitation)
-    source_term, fin = call(
-        functools.partial(scatter_source_kernel, count),
-        [SMEM] * 4 + [VMEM] * 10,
-        [((types, slices), F32), ((16, slices), F32)],
-        [pltpu.VMEM((events, slices), F32)],
-        flops=10**10,
-    )(weights, decay, place, marks, u, inverse, remain, misc, xtot, summaries, back, back_sums, sym, xrows)
-    excite_part, source_part = ring_sum(excite_term, source_term)
+    excite_part, source_part = ring_sum(
+        count, weights, decay, excite_term, flat, u, inverse, remain, xtot, summaries, back, back_sums, sym, xrows
+    )
+    comp = jnp.sum(back[:, count, :], axis=0)
     base_part = jnp.sum(base_parts, axis=0).reshape(types // peers)
 
     events_all = events * peers
     factor = types / events_all
-    grad_excite = factor * excite_part.T - fin[0][:, None] / events_all
-    grad_base = factor * base_part - fin[8, 0] / events_all
+    grad_excite = factor * excite_part.T - comp[:, None] / events_all
+    grad_base = factor * base_part - misc[8, 0] / events_all
     return grad_excite, factor * source_part.T, grad_base
 
 

time: 185 us -> 190 us (1.027)
  Pallas kernels: 161 us -> 165 us
    pallas_call x2 -> x1, Pallas kernels: 97.9 us -> 102 us  [ring_sum(): pl.pallas_call(functools.partial(ring_kernel, n, count), out_shape=[jax.S...]
    unnamed x52 -> x48, local copies, waits for them, and re-layouts: 20.8 us -> 19.7 us
where the time goes in v3:
time: 190 us; the launch traced here: 189 us
  Pallas kernels  165 us (87%)
  local copies, waits for them, and re-layouts  20.2 us (11%)
  other arithmetic  2.23 us (1%)
    pallas_call x1, Pallas kernels, ring_sum(): pl.pallas_call(functools.partial(ring_kernel, n, count), out_shape=[jax.S...  102 us
    pallas_call x3, Pallas kernels, exchange(): pl.pallas_call(functools.partial(exchange_kernel, axis, n, spread), out_s...  24.3 us
    unnamed x48, local copies, waits for them, and re-layouts  19.7 us
    pallas_call x1, Pallas kernels, body(): call(functools.partial(gather_kernel, count), [SMEM, SMEM, VMEM, VMEM, VM...  14.1 us
    pallas_call x1, Pallas kernels, body(): call(scatter_excite_kernel, [SMEM] + [VMEM] * 2, [((types, slices), F32)]...  13.5 us
    pallas_call x1, Pallas kernels, body(): call(functools.partial(inside_kernel, count), [SMEM, SMEM] + [VMEM] * 4,...  5.29 us
    pallas_call x1, Pallas kernels, body(): call(functools.partial(forward_kernel, count, rank), [SMEM, SMEM, SMEM] +...  4.21 us

profile of v3, /device:TPU:0, one launch (start us, length us, event | category | flops | bytes accessed | tf_op | source)
XLA Modules:
  0.0 188.8 jit_solution(1818007234353515245)
XLA Ops:
  0.6 1.6 copy-done.1
  2.2 1.6 copy-done.2
  3.8 0.7 copy-done.9
  4.5 0.7 copy-done.13
  5.9 14.1 %shard_map.94 = (f32[4096,128]{1,0:T(8,128)S(1)}, f32[4096,128]{1,0:T(8,128)S(1)}, f32[32,128]{1,0:T(8,128)S(1)}, f32[256,128]{1,0:T(8,128)S(1)}, f32[16,128]{1,0:T(8,128)S(1)}, /*index=5*/f32[8,128]{1,0:T(8,128)S(1)}) custom-call(s32[4096]{0:T(1024)S(1)} %copy-done.9, f32[8]{0:T(128)S(1)} %copy-done.15, s32[32,128]{1,0:T(8,128)S(1)} %bitcast.16, ...), custom_call_target="tpu_custom_call" | custom-call | flops 100000000 | bytes 4194304 | tf_op jit(solution)/shard_map/pallas_call | solution.py:480
  20.0 1.3 copy-done.5
  22.0 10.0 %shard_map.96.summaries = f32[8,16,128]{2,1,0:T(8,128)} custom-call(f32[16,128]{1,0:T(8,128)} %copy-done.18), custom_call_target="tpu_custom_call" | custom-call | tf_op jit(solution)/shard_map/pallas_call | solution.py:301
  32.0 1.6 copy-done.6
  33.6 5.3 %shard_map.95 = (f32[4096,128]{1,0:T(8,128)S(1)}, f32[4096,128]{1,0:T(8,128)S(1)}, bf16[4096,128]{1,0:T(8,128)(2,1)S(1)}, f32[32,128]{1,0:T(8,128)S(1)}) custom-call(f32[8]{0:T(128)S(1)} %copy-done.19, f32[8]{0:T(128)S(1)} %copy-done.16, f32[32,128]{1,0:T(8,128)S(1)} %get-tuple-element.25.u_ref, s32[32,128]{1,0:T(8,128)S(1)} %bitcast.12, ...), custom_call_target="tpu_custom_call" | custom-call | flops 5000000000 | bytes 4194304 | tf_op jit(solution)/shard_map/pallas_call | solution.py:487
  38.9 1.3 copy-done.3
  40.2 4.2 %shard_map.97 = (f32[4096,128]{1,0:T(8,128)S(1)}, f32[32,128]{1,0:T(8,128)S(1)}, f32[32,128]{1,0:T(8,128)S(1)}, f32[16,128]{1,0:T(8,128)S(1)}) custom-call(f32[8]{0:T(128)S(1)} %copy-done.19, f32[8]{0:T(128)S(1)} %copy-done.16, s32[1]{0:T(128)} %bitcast.3.place, f32[32,128]{1,0:T(8,128)S(1)} %get-tuple-element.25.u_ref, f32[8,16,128]{2,1,0:T(8,128)S(1)} %copy-done.7, ...), custom_call_target="tpu_custom_call" | custom-call | flops 100000000 | bytes 4194304 | tf_op jit(solution)/shard_map/pallas_call | solution.py:493
  45.1 1.3 copy-done.20
  47.6 5.1 %shard_map.98.total = f32[4,32,128]{2,1,0:T(8,128)} custom-call(f32[32,128]{1,0:T(8,128)} %copy-done.14), custom_call_target="tpu_custom_call" | custom-call | tf_op jit(solution)/shard_map/pallas_call | solution.py:301
  52.7 0.8 copy-done.8
  53.6 1.7 shard_map.99
  56.5 9.1 %shard_map.101 = (f32[8,16,128]{2,1,0:T(8,128)}, f32[8,8,128]{2,1,0:T(8,128)}) custom-call(f32[16,128]{1,0:T(8,128)} %copy-done.17, f32[8,8,128]{2,1,0:T(8,128)} %bitcast.15), custom_call_target="tpu_custom_call" | custom-call | tf_op jit(solution)/shard_map/pallas_call | solution.py:301
  65.6 0.8 reduce_sum.19
  67.0 0.8 slice_reduce_fusion
  67.8 1.6 copy-done.21
  69.3 13.5 %shard_map.100.x0 = f32[8192,128]{1,0:T(8,128)S(1)} custom-call(s32[4096]{0:T(1024)S(1)} %copy-done.10, f32[32,128]{1,0:T(8,128)S(1)} %get-tuple-element.35.inverse, f32[4096,128]{1,0:T(8,128)S(1)} %copy-done.21), custom_call_target="tpu_custom_call" | custom-call | flops 10000000000 | bytes 4194304 | tf_op jit(solution)/shard_map/pallas_call | solution.py:507
  82.8 1.9 %copy-done = f32[8192,128]{1,0:T(8,128)} copy-done((f32[8192,128]{1,0:T(8,128)}, f32[8192,128]{1,0:T(8,128)S(1)}, u32[]{:S(2)}) %copy-start) | copy-done | bytes 4194328
  84.8 102.0 %shard_map.102 = (f32[1024,128]{1,0:T(8,128)S(1)}, f32[1024,128]{1,0:T(8,128)S(1)}) custom-call(f32[8]{0:T(128)S(1)} %copy-done.19, f32[8]{0:T(128)S(1)} %copy-done.16, f32[8192,128]{1,0:T(8,128)} %copy-done, s32[32,128]{1,0:T(8,128)S(1)} %bitcast.14, f32[32,128]{1,0:T(8,128)S(1)} %get-tuple-element.25.u_ref, f32[32,128]{1,0:T(8,128)S(1)} %get-tuple-element.35.inverse, ...), custom_call_target="tpu_custom_call" | custom-call | tf_op jit(solution)/shard_map/pallas_call | solution.py:447
  186.8 1.0 copy.11
  187.8 1.0 copy.10
  (39 shorter events, 4.3 us)
Async XLA Ops:
  0.6 1.6 copy-start.1
  2.2 1.6 copy-start.2
  3.8 0.7 copy-start.9
  4.5 0.7 copy-start.13
  5.3 0.7 copy-start.15
  5.9 26.1 %copy-start.10 = (s32[4096]{0:T(1024)S(1)}, s32[4096]{0:T(1024)}, u32[]{:S(2)}) copy-start(s32[4096]{0:T(1024)} %marks.3) | copy-start | bytes 49156
  5.9 26.1 %copy-start.16 = (f32[8]{0:T(128)S(1)}, f32[8]{0:T(128)}, u32[]{:S(2)}) copy-start(f32[8]{0:T(128)} %decay.9) | copy-start | bytes 100
  5.9 26.1 %copy-start.19 = (f32[8]{0:T(128)S(1)}, f32[8]{0:T(128)}, u32[]{:S(2)}) copy-start(f32[8]{0:T(128)} %weights.5) | copy-start | bytes 100
  5.9 26.1 %copy-start.22 = (f32[8192]{0:T(1024)S(1)}, f32[8192]{0:T(1024)}, u32[]{:S(2)}) copy-start(f32[8192]{0:T(1024)} %param.11) | copy-start | bytes 98308
  20.0 1.4 copy-start.5
  21.4 0.6 copy-start.18
  32.0 1.6 copy-start.6
  33.6 6.6 %copy-start.7 = (f32[8,16,128]{2,1,0:T(8,128)S(1)}, f32[8,16,128]{2,1,0:T(8,128)}, u32[]{:S(2)}) copy-start(f32[8,16,128]{2,1,0:T(8,128)} %shard_map.96.summaries) | copy-start | bytes 196612
  38.9 1.3 copy-start.3
  44.5 0.6 copy-start.14
  45.1 1.3 copy-start.20
  52.7 0.8 copy-start.8
  55.2 0.6 copy-start.12
  55.9 0.6 copy-start.17
  67.7 1.6 copy-start.21
  69.3 15.4 %copy-start.4 = (f32[4096,128]{1,0:T(8,128)S(1)}, f32[4096,128]{1,0:T(8,128)}, u32[]{:S(2)}) copy-start(f32[4096,128]{1,0:T(8,128)} %copy-done.3) | copy-start | bytes 6291460
  69.3 15.4 %copy-start.11 = (f32[8,16,128]{2,1,0:T(8,128)S(1)}, f32[8,16,128]{2,1,0:T(8,128)}, u32[]{:S(2)}) copy-start(f32[8,16,128]{2,1,0:T(8,128)} %get-tuple-element.41.back) | copy-start | bytes 196612
  82.8 1.9 %copy-start = (f32[8192,128]{1,0:T(8,128)}, f32[8192,128]{1,0:T(8,128)S(1)}, u32[]{:S(2)}) copy-start(f32[8192,128]{1,0:T(8,128)S(1)} %shard_map.100.x0) | copy-start | bytes 12582916

commit v4 on v3

--- a/solution.py
+++ b/solution.py
@@ -414,8 +414,14 @@
         chunk(member(at + away * (2 * lax.rem(i, 2) - 1)))
         return 0
 
-    lax.fori_loop(1, n - 1, excite_step, 0)
+    def two_steps(p, _):
+        lax.fori_loop(2 * p + 1, 2 * p + 3, excite_step, 0)
+        step(p, (2, 3))
+        return 0
+
+    lax.fori_loop(1, 3, excite_step, 0)
     begin((2, 3))
+    lax.fori_loop(1, n // 2 - 1, two_steps, 0)
 
     def rest(i, _):
         chunk(member(at + i * (n // 2)))
@@ -428,7 +434,7 @@
         step(s, (2, 3))
         return 0
 
-    lax.fori_loop(1, n - 1, source_step, 0)
+    lax.fori_loop(n // 2 - 1, n - 1, source_step, 0)
     finish((2, 3))
 
     def sent(s, _):

time: 190 us -> 180 us (0.947)
  Pallas kernels: 165 us -> 155 us
    pallas_call x1, Pallas kernels: 102 us -> 91.9 us  [ring_sum(): pl.pallas_call(functools.partial(ring_kernel, n, count), out_shape=[jax.S...]
where the time goes in v4:
time: 180 us; the launch traced here: 179 us
  Pallas kernels  155 us (86%)
  local copies, waits for them, and re-layouts  20.2 us (11%)
  other arithmetic  2.23 us (1%)
    pallas_call x1, Pallas kernels, ring_sum(): pl.pallas_call(functools.partial(ring_kernel, n, count), out_shape=[jax.S...  91.9 us
    pallas_call x3, Pallas kernels, exchange(): pl.pallas_call(functools.partial(exchange_kernel, axis, n, spread), out_s...  24.3 us
    unnamed x48, local copies, waits for them, and re-layouts  19.7 us
    pallas_call x1, Pallas kernels, body(): call(functools.partial(gather_kernel, count), [SMEM, SMEM, VMEM, VMEM, VM...  14.1 us
    pallas_call x1, Pallas kernels, body(): call(scatter_excite_kernel, [SMEM] + [VMEM] * 2, [((types, slices), F32)]...  13.5 us
    pallas_call x1, Pallas kernels, body(): call(functools.partial(inside_kernel, count), [SMEM, SMEM] + [VMEM] * 4,...  5.29 us
    pallas_call x1, Pallas kernels, body(): call(functools.partial(forward_kernel, count, rank), [SMEM, SMEM, SMEM] +...  4.21 us

profile of v4, /device:TPU:0, one launch (start us, length us, event | category | flops | bytes accessed | tf_op | source)
XLA Modules:
  0.0 178.8 jit_solution(17179379099519403301)
XLA Ops:
  0.6 1.6 copy-done.1
  2.2 1.6 copy-done.2
  3.8 0.7 copy-done.9
  4.5 0.7 copy-done.13
  5.9 14.1 %shard_map.94 = (f32[4096,128]{1,0:T(8,128)S(1)}, f32[4096,128]{1,0:T(8,128)S(1)}, f32[32,128]{1,0:T(8,128)S(1)}, f32[256,128]{1,0:T(8,128)S(1)}, f32[16,128]{1,0:T(8,128)S(1)}, /*index=5*/f32[8,128]{1,0:T(8,128)S(1)}) custom-call(s32[4096]{0:T(1024)S(1)} %copy-done.9, f32[8]{0:T(128)S(1)} %copy-done.15, s32[32,128]{1,0:T(8,128)S(1)} %bitcast.16, ...), custom_call_target="tpu_custom_call" | custom-call | flops 100000000 | bytes 4194304 | tf_op jit(solution)/shard_map/pallas_call | solution.py:486
  20.0 1.3 copy-done.5
  22.0 10.0 %shard_map.96.summaries = f32[8,16,128]{2,1,0:T(8,128)} custom-call(f32[16,128]{1,0:T(8,128)} %copy-done.18), custom_call_target="tpu_custom_call" | custom-call | tf_op jit(solution)/shard_map/pallas_call | solution.py:301
  32.0 1.6 copy-done.6
  33.6 5.3 %shard_map.95 = (f32[4096,128]{1,0:T(8,128)S(1)}, f32[4096,128]{1,0:T(8,128)S(1)}, bf16[4096,128]{1,0:T(8,128)(2,1)S(1)}, f32[32,128]{1,0:T(8,128)S(1)}) custom-call(f32[8]{0:T(128)S(1)} %copy-done.19, f32[8]{0:T(128)S(1)} %copy-done.16, f32[32,128]{1,0:T(8,128)S(1)} %get-tuple-element.25.u_ref, s32[32,128]{1,0:T(8,128)S(1)} %bitcast.12, ...), custom_call_target="tpu_custom_call" | custom-call | flops 5000000000 | bytes 4194304 | tf_op jit(solution)/shard_map/pallas_call | solution.py:493
  38.9 1.3 copy-done.3
  40.2 4.2 %shard_map.97 = (f32[4096,128]{1,0:T(8,128)S(1)}, f32[32,128]{1,0:T(8,128)S(1)}, f32[32,128]{1,0:T(8,128)S(1)}, f32[16,128]{1,0:T(8,128)S(1)}) custom-call(f32[8]{0:T(128)S(1)} %copy-done.19, f32[8]{0:T(128)S(1)} %copy-done.16, s32[1]{0:T(128)} %bitcast.3.place, f32[32,128]{1,0:T(8,128)S(1)} %get-tuple-element.25.u_ref, f32[8,16,128]{2,1,0:T(8,128)S(1)} %copy-done.7, ...), custom_call_target="tpu_custom_call" | custom-call | flops 100000000 | bytes 4194304 | tf_op jit(solution)/shard_map/pallas_call | solution.py:499
  45.1 1.3 copy-done.20
  47.6 5.1 %shard_map.98.total = f32[4,32,128]{2,1,0:T(8,128)} custom-call(f32[32,128]{1,0:T(8,128)} %copy-done.14), custom_call_target="tpu_custom_call" | custom-call | tf_op jit(solution)/shard_map/pallas_call | solution.py:301
  52.7 0.8 copy-done.8
  53.6 1.7 shard_map.99
  56.5 9.1 %shard_map.101 = (f32[8,16,128]{2,1,0:T(8,128)}, f32[8,8,128]{2,1,0:T(8,128)}) custom-call(f32[16,128]{1,0:T(8,128)} %copy-done.17, f32[8,8,128]{2,1,0:T(8,128)} %bitcast.15), custom_call_target="tpu_custom_call" | custom-call | tf_op jit(solution)/shard_map/pallas_call | solution.py:301
  65.6 0.8 reduce_sum.19
  67.0 0.8 slice_reduce_fusion
  67.8 1.6 copy-done.21
  69.3 13.5 %shard_map.100.x0 = f32[8192,128]{1,0:T(8,128)S(1)} custom-call(s32[4096]{0:T(1024)S(1)} %copy-done.10, f32[32,128]{1,0:T(8,128)S(1)} %get-tuple-element.35.inverse, f32[4096,128]{1,0:T(8,128)S(1)} %copy-done.21), custom_call_target="tpu_custom_call" | custom-call | flops 10000000000 | bytes 4194304 | tf_op jit(solution)/shard_map/pallas_call | solution.py:513
  82.8 1.9 %copy-done = f32[8192,128]{1,0:T(8,128)} copy-done((f32[8192,128]{1,0:T(8,128)}, f32[8192,128]{1,0:T(8,128)S(1)}, u32[]{:S(2)}) %copy-start) | copy-done | bytes 4194328
  84.8 91.9 %shard_map.102 = (f32[1024,128]{1,0:T(8,128)S(1)}, f32[1024,128]{1,0:T(8,128)S(1)}) custom-call(f32[8]{0:T(128)S(1)} %copy-done.19, f32[8]{0:T(128)S(1)} %copy-done.16, f32[8192,128]{1,0:T(8,128)} %copy-done, s32[32,128]{1,0:T(8,128)S(1)} %bitcast.14, f32[32,128]{1,0:T(8,128)S(1)} %get-tuple-element.25.u_ref, f32[32,128]{1,0:T(8,128)S(1)} %get-tuple-element.35.inverse, ...), custom_call_target="tpu_custom_call" | custom-call | tf_op jit(solution)/shard_map/pallas_call | solution.py:453
  176.8 1.0 copy.11
  177.8 1.0 copy.10
  (39 shorter events, 4.3 us)
Async XLA Ops:
  0.6 1.6 copy-start.1
  2.2 1.6 copy-start.2
  3.8 0.7 copy-start.9
  4.5 0.7 copy-start.13
  5.3 0.7 copy-start.15
  5.9 26.1 %copy-start.10 = (s32[4096]{0:T(1024)S(1)}, s32[4096]{0:T(1024)}, u32[]{:S(2)}) copy-start(s32[4096]{0:T(1024)} %marks.3) | copy-start | bytes 49156
  5.9 26.1 %copy-start.16 = (f32[8]{0:T(128)S(1)}, f32[8]{0:T(128)}, u32[]{:S(2)}) copy-start(f32[8]{0:T(128)} %decay.9) | copy-start | bytes 100
  5.9 26.1 %copy-start.19 = (f32[8]{0:T(128)S(1)}, f32[8]{0:T(128)}, u32[]{:S(2)}) copy-start(f32[8]{0:T(128)} %weights.5) | copy-start | bytes 100
  5.9 26.1 %copy-start.22 = (f32[8192]{0:T(1024)S(1)}, f32[8192]{0:T(1024)}, u32[]{:S(2)}) copy-start(f32[8192]{0:T(1024)} %param.11) | copy-start | bytes 98308
  20.0 1.4 copy-start.5
  21.4 0.6 copy-start.18
  32.0 1.6 copy-start.6
  33.6 6.6 %copy-start.7 = (f32[8,16,128]{2,1,0:T(8,128)S(1)}, f32[8,16,128]{2,1,0:T(8,128)}, u32[]{:S(2)}) copy-start(f32[8,16,128]{2,1,0:T(8,128)} %shard_map.96.summaries) | copy-start | bytes 196612
  38.9 1.3 copy-start.3
  44.5 0.6 copy-start.14
  45.1 1.3 copy-start.20
  52.7 0.8 copy-start.8
  55.2 0.6 copy-start.12
  55.9 0.6 copy-start.17
  67.7 1.6 copy-start.21
  69.3 15.4 %copy-start.4 = (f32[4096,128]{1,0:T(8,128)S(1)}, f32[4096,128]{1,0:T(8,128)}, u32[]{:S(2)}) copy-start(f32[4096,128]{1,0:T(8,128)} %copy-done.3) | copy-start | bytes 6291460
  69.3 15.4 %copy-start.11 = (f32[8,16,128]{2,1,0:T(8,128)S(1)}, f32[8,16,128]{2,1,0:T(8,128)}, u32[]{:S(2)}) copy-start(f32[8,16,128]{2,1,0:T(8,128)} %get-tuple-element.41.back) | copy-start | bytes 196612
  82.8 1.9 %copy-start = (f32[8192,128]{1,0:T(8,128)}, f32[8192,128]{1,0:T(8,128)S(1)}, u32[]{:S(2)}) copy-start(f32[8192,128]{1,0:T(8,128)S(1)} %shard_map.100.x0) | copy-start | bytes 12582916
